TPU v7x, 32 devices: a whole 2x2x4 slice. The times are simulated.
32 devices in a mesh: seq: 8 (over z, y), tp: 2 (over x), dp: 2 (over core).
Axes of the slice: x: 2, y: 2, z: 4, core: 2. Of those that a mesh axis runs over, the one named last changes fastest.
Arguments:
- codes: int32 [2, 2048], P('dp', 'seq'), may hold values from 0 to 4095
- targets: int32 [2, 2048], P('dp', 'seq'), may hold values from 0 to 4095
- tok_weights: int32 [2, 2048], P('dp', 'seq'), may hold values from 1 to 4
- group_ids: int32 [2, 2048], P('dp'), may hold values from 0 to 19, as said below
- labels: int32 [2, 2], replicated, may hold values from 0 to 999
- tables_w: float32 [5106, 1024], P(None, ('seq', 'dp')), may hold values from -6 to 6
- tables_m: float32 [5106, 1024], P(None, ('seq', 'dp')), may hold values from -0.0014648438 to 0.0014648438, as said below
- tables_v: float32 [5106, 1024], P(None, ('seq', 'dp')), may hold values from 5.820766e-11 to 2.3841858e-07, as said below
- ada_w: float32 [1024, 8192], P(('seq', 'dp')), may hold values from -0.1875 to 0.1875
- ada_m: float32 [1024, 8192], P(('seq', 'dp')), may hold values from -0.00390625 to 0.00390625
- ada_v: float32 [1024, 8192], P(('seq', 'dp')), may hold values from 5.9604645e-08 to 2.3841858e-07
- attn_w: float32 [4, 1024, 1024], P(None, ('seq', 'dp'), 'tp'), may hold values from -0.75 to 0.75
- attn_m: float32 [4, 1024, 1024], P(None, ('seq', 'dp'), 'tp'), may hold values from -0.00390625 to 0.00390625
- attn_v: float32 [4, 1024, 1024], P(None, ('seq', 'dp'), 'tp'), may hold values from 5.9604645e-08 to 2.3841858e-07
- mlp_w: float32 [2, 1024, 4096], P(None, ('seq', 'dp'), 'tp'), may hold values from -0.1875 to 0.1875
- mlp_m: float32 [2, 1024, 4096], P(None, ('seq', 'dp'), 'tp'), may hold values from -0.00390625 to 0.00390625
- mlp_v: float32 [2, 1024, 4096], P(None, ('seq', 'dp'), 'tp'), may hold values from 5.9604645e-08 to 2.3841858e-07
- head_w: float32 [1024, 4096], P(('seq', 'dp'), 'tp'), may hold values from -0.1875 to 0.1875
- head_m: float32 [1024, 4096], P(('seq', 'dp'), 'tp'), may hold values from -0.00390625 to 0.00390625
- head_v: float32 [1024, 4096], P(('seq', 'dp'), 'tp'), may hold values from 5.9604645e-08 to 2.3841858e-07
- small_w: float32 [2, 1024], P(None, 'tp'), may hold values from -8 to 8
- small_m: float32 [2, 1024], P(None, 'tp'), may hold values from -0.00390625 to 0.00390625
- small_v: float32 [2, 1024], P(None, 'tp'), may hold values from 5.9604645e-08 to 2.3841858e-07
Outputs:
- loss: float32 [], replicated
- grad_norm: float32 [], replicated
- tables_m_new: float32 [5106, 1024], P(None, ('seq', 'dp'))
- tables_v_new: float32 [5106, 1024], P(None, ('seq', 'dp'))
- tables_w_new: float32 [5106, 1024], P(None, ('seq', 'dp'))
- ada_m_new: float32 [1024, 8192], P(('seq', 'dp'))
- ada_v_new: float32 [1024, 8192], P(('seq', 'dp'))
- ada_w_new: float32 [1024, 8192], P(('seq', 'dp'))
- attn_m_new: float32 [4, 1024, 1024], P(None, ('seq', 'dp'), 'tp')
- attn_v_new: float32 [4, 1024, 1024], P(None, ('seq', 'dp'), 'tp')
- attn_w_new: float32 [4, 1024, 1024], P(None, ('seq', 'dp'), 'tp')
- attn_bf: bfloat16 [4, 1024, 1024], P(None, ('seq', 'dp'), 'tp')
- mlp_m_new: float32 [2, 1024, 4096], P(None, ('seq', 'dp'), 'tp')
- mlp_v_new: float32 [2, 1024, 4096], P(None, ('seq', 'dp'), 'tp')
- mlp_w_new: float32 [2, 1024, 4096], P(None, ('seq', 'dp'), 'tp')
- mlp_bf: bfloat16 [2, 1024, 4096], P(None, ('seq', 'dp'), 'tp')
- head_m_new: float32 [1024, 4096], P(('seq', 'dp'), 'tp')
- head_v_new: float32 [1024, 4096], P(('seq', 'dp'), 'tp')
- head_w_new: float32 [1024, 4096], P(('seq', 'dp'), 'tp')
- head_bf: bfloat16 [1024, 4096], P(('seq', 'dp'), 'tp')
- small_m_new: float32 [2, 1024], P(None, 'tp')
- small_v_new: float32 [2, 1024], P(None, 'tp')
- small_w_new: float32 [2, 1024], P(None, 'tp')
Inputs may be any that keep to these rules, and one draw needn't show every extreme that they name: `group_ids`: each row holds 2 items of 1024 tokens, numbered in a rotation drawn for each row; tokens are ordered by scale, then by position of the item in the row; each item's scales follow one of VAR's two token plans (680 or 2240 tokens) scaled to its length, every scale 0 nonempty. `tables_m`: first moments of the tables, smaller on the code rows. `tables_v`: positive second moments of the tables, smaller on the code rows.
All inputs are finite; a program needn't handle non-finite values.
Results may differ from a plain program's by a relative error of at most 0.0035.
The roundings to bfloat16 on the way count: a program that leaves them out, or rounds other values in their place, can miss the bound.
Values may be sent and summed in bfloat16 or wider, within the bound.
A program may use at most 320 MiB of HBM per device.

v0:
```python
import jax
import jax.numpy as jnp
from jax import lax
from jax.sharding import PartitionSpec as P

HD = 64
V = 4096
NCLS = 1000
LEVELS = 10
STEP = 3


highest = lax.Precision.HIGHEST


def combined_all(value, axis, join):
    pieces = jax.tree.map(lambda part: lax.all_gather(part, axis), value)
    head = jax.tree.map(lambda part: part[0], pieces)
    tail = jax.tree.map(lambda part: part[1:], pieces)
    running, _ = lax.scan(lambda running, share: (join(running, share), None), head, tail)
    return running


def layer_mod(resid, shift, scale):
    centered = resid - jnp.mean(resid, -1, keepdims=True)
    normed = centered * lax.rsqrt(jnp.mean(centered * centered, -1, keepdims=True) + 1e-06)
    return normed * (1.0 + scale) + shift


def unit_rows(value):
    return value * lax.rsqrt(jnp.mean(value * value, -1, keepdims=True) + 1e-06)


def query_scale(value):
    return unit_rows(value) * 0.25


def gelu_tanh(value):
    return jax.nn.gelu(value, approximate=True)


def contract(left, right, left_dim, right_dim):
    return lax.dot_general(
        left, right, (((left_dim,), (right_dim,)), ((), ())), preferred_element_type=jnp.float32
    )


def tp_total(value):
    return lax.psum(value, "tp")


def allowed_mask(query_groups, key_groups):
    same = query_groups[:, None] // LEVELS == key_groups[None, :] // LEVELS
    return same & (key_groups[None, :] <= query_groups[:, None])


def head_slice(value, index):
    return lax.dynamic_index_in_dim(value, index, 1, keepdims=False)


def joined_heads(value):
    return jnp.transpose(value, (1, 0, 2)).reshape(value.shape[1], -1)


def stats_combine(first, second):
    top = jnp.maximum(first[0], second[0])
    total = first[1] * jnp.exp(first[0] - top) + second[1] * jnp.exp(second[0] - top)
    return (top, total, first[2] + second[2])


def adamw(weight, first, second, grad, rate):
    first = 0.5 * first + 0.5 * grad
    second = 0.5 * second + 0.5 * grad * grad
    fix = 1.0 - 0.5**STEP
    update = first / fix / (jnp.sqrt(second / fix) + 1e-08)
    return (first, second, weight - rate * (update + 0.05 * weight))


def layer_forward(resid, mod_parts, attn, mlp, small, groups_own, groups_all):
    tokens = resid.shape[0]
    heads = small.shape[1] // HD
    h_one = layer_mod(resid, mod_parts[0], mod_parts[1]).astype(jnp.bfloat16)
    project = jnp.einsum("td,kdc->ktc", h_one, attn[:3], preferred_element_type=jnp.float32)
    q_raw = (project[0] + small[0]).reshape(tokens, heads, HD)
    k_raw = project[1].reshape(tokens, heads, HD)
    queries = query_scale(q_raw).astype(jnp.bfloat16)
    keys = unit_rows(k_raw).astype(jnp.bfloat16).reshape(tokens, -1)
    values = (project[2] + small[1]).astype(jnp.bfloat16)
    keys_all, values_all = (
        lax.all_gather(keys, "seq", axis=0, tiled=True),
        lax.all_gather(values, "seq", axis=0, tiled=True),
    )
    rows_all = keys_all.shape[0]
    keys_all = keys_all.reshape(rows_all, heads, HD)
    values_all = values_all.reshape(rows_all, heads, HD)
    mask = allowed_mask(groups_own, groups_all)

    def forward_head(index):
        scores = jnp.where(
            mask, contract(head_slice(queries, index), head_slice(keys_all, index), 1, 1), -1e30
        )
        top = jnp.max(scores, 1, keepdims=True)
        expd = jnp.exp(scores - top)
        total = jnp.sum(expd, 1, keepdims=True)
        probs = (expd / total).astype(jnp.bfloat16)
        return (
            jnp.dot(probs, head_slice(values_all, index), preferred_element_type=jnp.float32),
            (top + jnp.log(total))[:, 0],
        )

    outs, log_totals = lax.map(forward_head, jnp.arange(heads))
    heads_out = joined_heads(outs).astype(jnp.bfloat16)
    attn_out = tp_total(contract(heads_out, attn[3], 1, 1))
    x_one = resid + mod_parts[2] * attn_out
    h_two = layer_mod(x_one, mod_parts[3], mod_parts[4]).astype(jnp.bfloat16)
    up_val = jnp.dot(h_two, mlp[0], preferred_element_type=jnp.float32)
    act = gelu_tanh(up_val).astype(jnp.bfloat16)
    mlp_out = tp_total(contract(act, mlp[1], 1, 1))
    x_two = x_one + mod_parts[5] * mlp_out
    saved = dict(
        resid=resid,
        h_one=h_one,
        q_raw=q_raw,
        k_raw=k_raw,
        queries=queries,
        keys_own=keys.reshape(tokens, heads, HD),
        values_own=values.reshape(tokens, heads, HD),
        keys_all=keys_all,
        values_all=values_all,
        mask=mask,
        log_totals=log_totals,
        heads_out=heads_out,
        attn_out=attn_out,
        x_one=x_one,
        h_two=h_two,
        up_val=up_val,
        act=act,
        mlp_out=mlp_out,
    )
    return (x_two, saved)


def layer_backward(d_x_two, saved, mod_parts, attn, mlp, small):
    tokens = d_x_two.shape[0]
    heads = small.shape[1] // HD
    d_mlp = (d_x_two * mod_parts[5]).astype(jnp.bfloat16)
    d_gate_two = d_x_two * saved["mlp_out"]
    grad_down = contract(d_mlp, saved["act"], 0, 0)
    d_act = jnp.dot(d_mlp, mlp[1], preferred_element_type=jnp.float32)
    d_up = jax.vjp(gelu_tanh, saved["up_val"])[1](d_act)[0].astype(jnp.bfloat16)
    grad_up = contract(saved["h_two"], d_up, 0, 0)
    d_h_two = tp_total(contract(d_up, mlp[0], 1, 1))
    d_x_one, d_shift_two, d_scale_two = jax.vjp(
        layer_mod, saved["x_one"], mod_parts[3], mod_parts[4]
    )[1](d_h_two)
    d_x_one = d_x_one + d_x_two
    d_attn = (d_x_one * mod_parts[2]).astype(jnp.bfloat16)
    d_gate_one = d_x_one * saved["attn_out"]
    grad_out = contract(d_attn, saved["heads_out"], 0, 0)
    d_heads = jnp.dot(d_attn, attn[3], preferred_element_type=jnp.float32).astype(jnp.bfloat16)
    d_heads3 = d_heads.reshape(tokens, heads, HD)
    queries = saved["queries"]
    keys_all = saved["keys_all"]
    values_all = saved["values_all"]
    log_totals = saved["log_totals"]
    mask = saved["mask"]

    def query_grads(index):
        key = head_slice(keys_all, index)
        scores = jnp.where(mask, contract(head_slice(queries, index), key, 1, 1), -1e30)
        probs = jnp.exp(scores - log_totals[index][:, None])
        d_probs = contract(head_slice(d_heads3, index), head_slice(values_all, index), 1, 1)
        delta = jnp.sum(probs * d_probs, 1)
        d_scores = (probs * (d_probs - delta[:, None])).astype(jnp.bfloat16)
        return (jnp.dot(d_scores, key, preferred_element_type=jnp.float32), delta)

    d_query, deltas = lax.map(query_grads, jnp.arange(heads))
    mask_part = lax.slice_in_dim(mask, 0, tokens * lax.axis_size("seq"), axis=1)
    keys_part = lax.slice_in_dim(keys_all, 0, tokens * lax.axis_size("seq"), axis=0)
    values_part = lax.slice_in_dim(values_all, 0, tokens * lax.axis_size("seq"), axis=0)

    def per_head(index):
        query = head_slice(queries, index)
        d_out = head_slice(d_heads3, index)
        scores = jnp.where(mask_part, contract(query, head_slice(keys_part, index), 1, 1), -1e30)
        probs = jnp.exp(scores - log_totals[index][:, None])
        d_probs = contract(d_out, head_slice(values_part, index), 1, 1)
        d_scores = (probs * (d_probs - deltas[index][:, None])).astype(jnp.bfloat16)
        return (contract(d_scores, query, 0, 0), contract(probs.astype(jnp.bfloat16), d_out, 0, 0))

    part_keys, part_values = lax.map(per_head, jnp.arange(heads))
    key_sums = lax.psum_scatter(
        jnp.concatenate([joined_heads(part_keys), joined_heads(part_values)], 1),
        "seq",
        scatter_dimension=0,
        tiled=True,
    )
    width = heads * HD
    d_keys_own = key_sums[:, :width].reshape(tokens, heads, HD)
    d_q_raw = jax.vjp(query_scale, saved["q_raw"])[1](jnp.transpose(d_query, (1, 0, 2)))[0]
    d_k_raw = jax.vjp(unit_rows, saved["k_raw"])[1](d_keys_own)[0]
    stacked = jnp.stack(
        [d_q_raw.reshape(tokens, -1), d_k_raw.reshape(tokens, -1), key_sums[:, width:]]
    ).astype(jnp.bfloat16)
    grad_qkv = jnp.einsum(
        "td,ktc->kdc", saved["h_one"], stacked, preferred_element_type=jnp.float32
    )
    bias_grad = jnp.stack(
        [jnp.sum(stacked[0].astype(jnp.float32), 0), jnp.sum(stacked[2].astype(jnp.float32), 0)]
    )
    d_h_one = tp_total(
        jnp.einsum("ktc,kdc->td", stacked, attn[:3], preferred_element_type=jnp.float32)
    )
    d_resid, d_shift_one, d_scale_one = jax.vjp(
        layer_mod, saved["resid"], mod_parts[0], mod_parts[1]
    )[1](d_h_one)
    d_resid = d_resid + d_x_one
    d_mods = [d_shift_one, d_scale_one, d_gate_one, d_shift_two, d_scale_two, d_gate_two]
    grad_attn = jnp.concatenate([grad_qkv, grad_out[None]], 0)
    grad_mlp = jnp.stack([grad_up, grad_down])
    return (d_resid, d_mods, grad_attn, grad_mlp, bias_grad)


def per_device(
    codes,
    targets,
    tok_weights,
    group_ids,
    labels,
    tables_w,
    tables_m,
    tables_v,
    ada_w,
    ada_m,
    ada_v,
    attn_w,
    attn_m,
    attn_v,
    mlp_w,
    mlp_m,
    mlp_v,
    head_w,
    head_m,
    head_v,
    small_w,
    small_m,
    small_v,
):
    tables, ada, attn, mlp, head = (
        lax.all_gather(tables_w.astype(jnp.bfloat16), ("seq", "dp"), axis=1, tiled=True),
        lax.all_gather(ada_w.astype(jnp.bfloat16), ("seq", "dp"), axis=0, tiled=True),
        lax.all_gather(attn_w.astype(jnp.bfloat16), ("seq", "dp"), axis=1, tiled=True),
        lax.all_gather(mlp_w.astype(jnp.bfloat16), ("seq", "dp"), axis=1, tiled=True),
        lax.all_gather(head_w.astype(jnp.bfloat16), ("seq", "dp"), axis=0, tiled=True),
    )
    tokens = codes.shape[1]
    groups_all = group_ids[0]
    groups_own = lax.dynamic_slice_in_dim(groups_all, lax.axis_index("seq") * tokens, tokens)
    row_index = lax.axis_index("dp")
    item_count = labels.shape[1]
    cond_all = tables[V + labels].astype(jnp.float32)
    silu_all = jax.nn.silu(cond_all).astype(jnp.bfloat16)
    cond_own = lax.dynamic_index_in_dim(cond_all, row_index, 0, keepdims=False)
    silu_own = lax.dynamic_index_in_dim(silu_all, row_index, 0, keepdims=False)
    label_own = lax.dynamic_index_in_dim(labels, row_index, 0, keepdims=False)
    select = (groups_own[:, None] // LEVELS == jnp.arange(item_count)[None, :]).astype(jnp.float32)
    mods_items = jnp.dot(silu_own, ada, preferred_element_type=jnp.float32)
    mod_parts = jnp.split(jnp.dot(select, mods_items, precision=highest), 8, axis=1)
    level_rows = V + NCLS + groups_own % LEVELS
    resid = tables[codes[0]].astype(jnp.float32) + tables[level_rows].astype(jnp.float32)
    x_two, saved = layer_forward(resid, mod_parts, attn, mlp, small_w, groups_own, groups_all)
    h_three = layer_mod(x_two, mod_parts[6], mod_parts[7]).astype(jnp.bfloat16)
    logits = jnp.dot(h_three, head, preferred_element_type=jnp.float32)
    vocab_part = head.shape[1]
    hit = (
        targets[0][:, None] - lax.axis_index("tp") * vocab_part == jnp.arange(vocab_part)[None, :]
    ).astype(jnp.float32)
    local_top = jnp.max(logits, 1)
    local_sum = jnp.sum(jnp.exp(logits - local_top[:, None]), 1)
    linear_part = 0.9 * jnp.sum(hit * logits, 1) + 0.1 / V * jnp.sum(logits, 1)
    top, total, linear_total = combined_all(
        (local_top, local_sum, linear_part), "tp", stats_combine
    )
    log_total = top + jnp.log(total)
    token_loss = log_total - linear_total
    weights = tok_weights[0].astype(jnp.float32)
    loss_part, weight_total = lax.psum(
        (jnp.sum(weights * token_loss), jnp.sum(weights)), ("seq", "dp")
    )
    loss = 128.0 * loss_part / weight_total
    scale_rows = 128.0 * weights / weight_total
    probs_v = jnp.exp(logits - log_total[:, None])
    d_logits = (scale_rows[:, None] * (probs_v - 0.9 * hit - 0.1 / V)).astype(jnp.bfloat16)
    grad_head = contract(h_three, d_logits, 0, 0)
    d_h_three = tp_total(contract(d_logits, head, 1, 1))
    d_x_two, d_shift_three, d_scale_three = jax.vjp(layer_mod, x_two, mod_parts[6], mod_parts[7])[
        1
    ](d_h_three)
    d_resid, d_mods, grad_attn, grad_mlp, bias_grad = layer_backward(
        d_x_two, saved, mod_parts, attn, mlp, small_w
    )
    d_tok_mods = jnp.concatenate(d_mods + [d_shift_three, d_scale_three], 1)
    d_mods_items = lax.dot_general(
        select,
        d_tok_mods,
        (((0,), (0,)), ((), ())),
        precision=highest,
        preferred_element_type=jnp.float32,
    )
    d_silu = jnp.dot(d_mods_items, ada.T, precision=highest, preferred_element_type=jnp.float32)
    d_cond = jax.vjp(jax.nn.silu, cond_own)[1](d_silu)[0]
    row_ids = jnp.concatenate([codes[0], level_rows, V + label_own])
    table_terms = jnp.concatenate([d_resid, d_resid, d_cond], 0)
    grad_tables = jax.ops.segment_sum(table_terms, row_ids, num_segments=tables.shape[0])
    g_tables = lax.psum_scatter(grad_tables, ("seq", "dp"), scatter_dimension=1, tiled=True)
    grad_ada = lax.dot_general(
        silu_own.astype(jnp.float32),
        d_mods_items,
        (((0,), (0,)), ((), ())),
        precision=highest,
        preferred_element_type=jnp.float32,
    )
    g_ada, g_attn, g_mlp, g_head = (
        lax.psum_scatter(grad_ada, ("seq", "dp"), scatter_dimension=0, tiled=True),
        lax.psum_scatter(grad_attn, ("seq", "dp"), scatter_dimension=1, tiled=True),
        lax.psum_scatter(grad_mlp, ("seq", "dp"), scatter_dimension=1, tiled=True),
        lax.psum_scatter(grad_head, ("seq", "dp"), scatter_dimension=0, tiled=True),
    )
    g_small = lax.psum(bias_grad, ("seq", "dp"))
    tp_count = lax.axis_size("tp")
    data_count = lax.axis_size("seq") * lax.axis_size("dp")
    local_squares = (jnp.sum(g_tables * g_tables) + jnp.sum(g_ada * g_ada)) / tp_count
    local_squares = (
        local_squares + jnp.sum(g_attn * g_attn) + jnp.sum(g_mlp * g_mlp) + jnp.sum(g_head * g_head)
    )
    local_squares = local_squares + jnp.sum(g_small * g_small) / data_count
    grad_norm = jnp.sqrt(lax.psum(local_squares, ("seq", "tp", "dp")))
    factor = jnp.minimum(1.0, 1.0 / (grad_norm + 1e-06))
    tables_n = adamw(tables_w, tables_m, tables_v, g_tables * factor, 0.3)
    ada_n = adamw(ada_w, ada_m, ada_v, g_ada * factor, 0.03)
    attn_n = adamw(attn_w, attn_m, attn_v, g_attn * factor, 0.1)
    mlp_n = adamw(mlp_w, mlp_m, mlp_v, g_mlp * factor, 0.02)
    head_n = adamw(head_w, head_m, head_v, g_head * factor, 0.03)
    small_n = adamw(small_w, small_m, small_v, g_small * factor, 0.5)
    return (
        loss,
        grad_norm,
        tables_n[0],
        tables_n[1],
        tables_n[2],
        ada_n[0],
        ada_n[1],
        ada_n[2],
        attn_n[0],
        attn_n[1],
        attn_n[2],
        attn_n[2].astype(jnp.bfloat16),
        mlp_n[0],
        mlp_n[1],
        mlp_n[2],
        mlp_n[2].astype(jnp.bfloat16),
        head_n[0],
        head_n[1],
        head_n[2],
        head_n[2].astype(jnp.bfloat16),
        small_n[0],
        small_n[1],
        small_n[2],
    )


def solution(mesh):
    placed = (
        P("dp", "seq"),
        P("dp", "seq"),
        P("dp", "seq"),
        P("dp", None),
        P(),
        P(None, ("seq", "dp")),
        P(None, ("seq", "dp")),
        P(None, ("seq", "dp")),
        P(("seq", "dp"), None),
        P(("seq", "dp"), None),
        P(("seq", "dp"), None),
        P(None, ("seq", "dp"), "tp"),
        P(None, ("seq", "dp"), "tp"),
        P(None, ("seq", "dp"), "tp"),
        P(None, ("seq", "dp"), "tp"),
        P(None, ("seq", "dp"), "tp"),
        P(None, ("seq", "dp"), "tp"),
        P(("seq", "dp"), "tp"),
        P(("seq", "dp"), "tp"),
        P(("seq", "dp"), "tp"),
        P(None, "tp"),
        P(None, "tp"),
        P(None, "tp"),
    )
    return jax.shard_map(
        per_device,
        mesh=mesh,
        in_specs=placed,
        out_specs=(
            P(),
            P(),
            P(None, ("seq", "dp")),
            P(None, ("seq", "dp")),
            P(None, ("seq", "dp")),
            P(("seq", "dp"), None),
            P(("seq", "dp"), None),
            P(("seq", "dp"), None),
            P(None, ("seq", "dp"), "tp"),
            P(None, ("seq", "dp"), "tp"),
            P(None, ("seq", "dp"), "tp"),
            P(None, ("seq", "dp"), "tp"),
            P(None, ("seq", "dp"), "tp"),
            P(None, ("seq", "dp"), "tp"),
            P(None, ("seq", "dp"), "tp"),
            P(None, ("seq", "dp"), "tp"),
            P(("seq", "dp"), "tp"),
            P(("seq", "dp"), "tp"),
            P(("seq", "dp"), "tp"),
            P(("seq", "dp"), "tp"),
            P(None, "tp"),
            P(None, "tp"),
            P(None, "tp"),
        ),
        check_vma=False,
    )
```

profile of v0, /device:TPU:0, one launch (start us, length us, event | category | flops | bytes accessed | tf_op | source)
XLA Modules:
  0.0 2208.4 jit_solution(4318916262440893668)
XLA Ops:
  12.5 89.0 %all-gather.14.cloned.1.call-done = bf16[5106,1024]{0,1:T(8,128)(2,1)} async-done(((bf16[5106,64]{0,1:T(8,128)(2,1)}), bf16[5106,1024]{0,1:T(8,128)(2,1)}) %all-gather.14.cloned.1.call-update) | async-done | bytes 10457104 | tf_op jit(solution)/shard_map/all_gather | solution.py:250
  101.5 14.4 copy.123
  115.9 6.9 gather_fusion
  122.8 7.1 gather_fusion.1
  130.0 6.1 gather_fusion.2
  136.7 92.7 %all-gather.16.cloned.1.call-done = bf16[1024,8192]{1,0:T(8,128)(2,1)} async-done(((bf16[64,8192]{1,0:T(8,128)(2,1)}), bf16[1024,8192]{1,0:T(8,128)(2,1)}) %all-gather.16.cloned.1.call-update) | async-done | bytes 16777232 | tf_op jit(solution)/shard_map/all_gather | solution.py:251
  229.3 8.0 fusion.128
  244.8 36.1 %all-gather.18.cloned.1.call-done = bf16[4,1024,512]{2,1,0:T(8,128)(2,1)} async-done(((bf16[4,64,512]{2,1,0:T(8,128)(2,1)}), bf16[4,1024,512]{2,1,0:T(8,128)(2,1)}) %all-gather.18.cloned.1.call-update) | async-done | bytes 4194320 | tf_op jit(solution)/shard_map/all_gather | solution.py:252
  289.0 45.9 %all-gather.20.cloned.1.call-done = bf16[2048,512]{1,0:T(8,128)(2,1)} async-done(((bf16[256,512]{1,0:T(8,128)(2,1)}), bf16[2048,512]{1,0:T(8,128)(2,1)}) %all-gather.20.cloned.1.call-update) | async-done | bytes 2097168 | tf_op jit(solution)/shard_map/all_gather | solution.py:90
  334.9 3.9 copy.129
  338.8 46.4 %all-gather.22.cloned.1.call-done = bf16[2048,512]{1,0:T(8,128)(2,1)} async-done(((bf16[256,512]{1,0:T(8,128)(2,1)}), bf16[2048,512]{1,0:T(8,128)(2,1)}) %all-gather.22.cloned.1.call-update) | async-done | bytes 2097168 | tf_op jit(solution)/shard_map/all_gather | solution.py:91
  389.2 49.5 %while.48 = (s32[]{:T(128)}, bf16[8,256,64]{1,2,0:T(8,128)(2,1)S(1)}, f32[8,256]{1,0:T(8,128)S(1)}, s32[8]{0:T(128)S(1)}, bf16[256,8,64]{0,2,1:T(8,128)(2,1)}, /...) while((s32[]{:T(128)}, ...), condition=%wide.region_7.8_spmd.clone.clone, body=%wide.region_4.7_spmd.clone.sunk.clone | while | flops 139460352 | bytes 6944419 | solution.py:111
  442.5 37.7 %all-reduce.9.cloned.1.call-done = f32[256,1024]{1,0:T(8,128)} async-done(((f32[256,1024]{1,0:T(8,128)}), f32[256,1024]{1,0:T(8,128)}) %all-reduce.9.cloned.1.call-update) | async-done | bytes 1048592 | tf_op jit(solution)/shard_map/psum | solution.py:49
  484.2 74.0 %all-gather.24.cloned.1.call-done = bf16[2,1024,2048]{2,1,0:T(8,128)(2,1)} async-done(((bf16[2,64,2048]{2,1,0:T(8,128)(2,1)}), bf16[2,1024,2048]{2,1,0:T(8,128)(2,1)}) %all-gather.24.cloned.1.call-update) | async-done | bytes 8388624 | tf_op jit(solution)/shard_map/all_gather | solution.py:253
  563.0 4.7 fusion.67
  569.2 31.6 %psum.66 = f32[]{:T(128)} all-reduce(f32[]{:T(128)} %convert_reduce_fusion.2), channel_id=1, replica_groups=mesh['seq'=8,'tp'=2,'dp'=2] {'seq','dp'}, use_global_device_ids=true, to_apply=%region_21.22 | all-reduce | flops 1 | bytes 8 | tf_op jit(solution)/shard_map/psum | solution.py:287
  600.8 5.4 all-reduce.11.cloned.1.call-done
  610.1 49.4 %all-gather.26.cloned.1.call-done = bf16[1024,2048]{1,0:T(8,128)(2,1)} async-done(((bf16[64,2048]{1,0:T(8,128)(2,1)}), bf16[1024,2048]{1,0:T(8,128)(2,1)}) %all-gather.26.cloned.1.call-update) | async-done | bytes 4194320 | tf_op jit(solution)/shard_map/all_gather | solution.py:254
  664.0 4.2 all-gather.4
  668.2 4.2 all-gather.5
  672.5 4.6 all-gather.3
  680.9 38.7 %all-reduce.13.cloned.1.call-done = f32[256,1024]{1,0:T(8,128)} async-done(((f32[256,1024]{1,0:T(8,128)}), f32[256,1024]{1,0:T(8,128)}) %all-reduce.13.cloned.1.call-update) | async-done | bytes 1048592 | tf_op jit(solution)/shard_map/psum | solution.py:49
  725.5 4.9 fusion.83
  733.8 40.1 %all-reduce.15.cloned.1.call-done = f32[256,1024]{1,0:T(8,128)} async-done(((f32[256,1024]{1,0:T(8,128)}), f32[256,1024]{1,0:T(8,128)}) %all-reduce.15.cloned.1.call-update) | async-done | bytes 1048592 | tf_op jit(solution)/shard_map/psum | solution.py:49
  782.6 59.2 %while.49 = (s32[]{:T(128)}, f32[8,256,64]{1,2,0:T(8,128)S(1)}, f32[8,256]{1,0:T(8,128)S(1)}, s32[8]{0:T(128)S(1)}, bf16[256,8,64]{0,2,1:T(8,128)(2,1)}, /*index...) while((s32[]{:T(128)}, f32[8,256,64]{1,2,0:T(8,128)S(1)}, ...), condition=%wide.region_30.31_spmd.clone.clone, body=%wide.region_28.30_spmd.clone.sunk.clone | while | flops 206569216 | bytes 11431607 | solution.py:177
  842.6 62.0 %while.50 = (s32[]{:T(128)}, f32[8,2048,64]{1,2,0:T(8,128)}, f32[8,2048,64]{1,2,0:T(8,128)}, s32[8]{0:T(128)S(1)}, bf16[256,8,64]{0,2,1:T(8,128)(2,1)}, /*index=...) while((s32[]{:T(128)}, f32[8,2048,64]{1,2,0:T(8,128)}, ...), condition=%wide.region_33.34_spmd.clone.clone, body=%wide.region_32.33_spmd.clone.sunk.clone | while | flops 273154048 | bytes 8023739 | solution.py:191
  904.6 5.4 copy.132
  910.0 5.3 copy.133
  915.3 8.2 pad_maximum_fusion.1
  925.9 146.8 %reduce-scatter.8.cloned.1.call-done = f32[256,1024]{1,0:T(8,128)} async-done(((f32[2048,1024]{1,0:T(8,128)}), f32[256,1024]{1,0:T(8,128)}) %reduce-scatter.8.cloned.1.call-update) | async-done | bytes 1048592 | tf_op jit(solution)/shard_map/reduce_scatter | solution.py:192
  1077.2 4.1 fusion.88
  1081.4 6.0 fusion.142
  1090.0 4.1 pad_maximum_fusion.2
  1094.1 10.2 copy.140
  1109.0 6.1 pad_maximum_fusion
  1115.7 4.8 all-reduce.17.cloned.1.call-done
  1132.3 13.4 fusion.118
  1145.8 18.5 scatter_custom_fusion
  1164.2 20.0 copy.145
  1184.4 17.3 fusion.126
  1203.8 25.3 %reduce-scatter.14.cloned.1.call-done = f32[64,2048]{1,0:T(8,128)} async-done(((f32[1024,2048]{1,0:T(8,128)}), f32[64,2048]{1,0:T(8,128)}) %reduce-scatter.14.cloned.1.call-update) | async-done | bytes 524304 | tf_op jit(solution)/shard_map/reduce_scatter | solution.py:327
  1230.9 35.1 %all-reduce.1 = (f32[]{:T(128)}, f32[2,512]{1,0:T(2,128)S(1)}) all-reduce(f32[]{:T(128)} %get-tuple-element.481, f32[2,512]{1,0:T(2,128)S(1)} %pad_maximum_fusion.6), channel_id=1, replica_groups=mesh['seq'=8,'tp'=2,'dp'=2] {'seq','dp'}, use_global_device_ids=true, to_apply=%region_19.20 | all-reduce | flops 1025 | bytes 8200 | tf_op jit(solution)/shard_map/psum | solution.py:287
  1267.9 135.0 %all-reduce.19.cloned.1.call-done = f32[4,1024,512]{2,0,1:T(4,128)} async-done(((f32[4,1024,512]{2,0,1:T(4,128)}), f32[4,1024,512]{2,0,1:T(4,128)}) %all-reduce.19.cloned.1.call-update) | async-done | bytes 8388624
  1404.8 181.0 %reduce-scatter.12.cloned.1.call-done = f32[2,64,2048]{2,1,0:T(8,128)} async-done(((f32[2,1024,2048]{2,1,0:T(8,128)}), f32[2,64,2048]{2,1,0:T(8,128)}) %reduce-scatter.12.cloned.1.call-update) | async-done | bytes 1048592 | tf_op jit(solution)/shard_map/reduce_scatter | solution.py:326
  1587.9 212.3 %reduce-scatter.16.cloned.1.call-done = f32[64,5106]{1,0:T(8,128)} async-done(((f32[1024,5106]{1,0:T(8,128)}), f32[64,5106]{1,0:T(8,128)}) %reduce-scatter.16.cloned.1.call-update) | async-done | bytes 1307152
  1806.3 330.5 %reduce-scatter.10.cloned.1.call-done = f32[64,8192]{1,0:T(8,128)} async-done(((f32[1024,8192]{1,0:T(8,128)}), f32[64,8192]{1,0:T(8,128)}) %reduce-scatter.10.cloned.1.call-update) | async-done | bytes 2097168 | tf_op jit(solution)/shard_map/reduce_scatter | solution.py:324
  2143.6 38.9 %psum.71 = f32[]{:T(128)} all-reduce(f32[]{:T(128)S(6)} %add.499), channel_id=1, replica_groups=mesh['seq'=8,'tp'=2,'dp'=2] {'seq','tp','dp'}, use_global_device_ids=true, to_apply=%region_54.55 | all-reduce | flops 1 | bytes 8 | tf_op jit(solution)/shard_map/psum | solution.py:337
  2192.2 3.9 multiply_subtract_fusion
  (495 shorter events, 247.9 us)
Async XLA Ops:
  7.2 94.3 %all-gather.14.cloned.1.call-start = ((), (), s32[]{:S(2)}) async-start(), calls=%async_computation.5 | async-start | bytes 11141120 | tf_op jit(solution)/shard_map/all_gather | solution.py:250
  9.7 219.6 %all-gather.16.cloned.1.call-start = ((), (), s32[]{:S(2)}) async-start(), calls=%async_computation.6 | async-start | bytes 17825792 | tf_op jit(solution)/shard_map/all_gather | solution.py:251
  10.9 270.0 %all-gather.18.cloned.1.call-start = ((), (), s32[]{:S(2)}) async-start(), calls=%async_computation.7 | async-start | bytes 4456448 | tf_op jit(solution)/shard_map/all_gather | solution.py:252
  11.7 323.2 %all-gather.20.cloned.1.call-start = ((), (), s32[]{:S(2)}) async-start(), calls=%async_computation.8 | async-start | bytes 2359296 | tf_op jit(solution)/shard_map/all_gather | solution.py:90
  122.8 118.3 %copy-start.3 = (bf16[256,1024]{1,0:T(8,128)(2,1)}, bf16[256,1024]{1,0:T(8,128)(2,1)S(1)}, u32[]{:S(2)}) copy-start(bf16[256,1024]{1,0:T(8,128)(2,1)S(1)} %gather_fusion) | copy-start | bytes 1572868
  129.9 111.2 %copy-start.6 = (bf16[256,1024]{1,0:T(8,128)(2,1)}, bf16[256,1024]{1,0:T(8,128)(2,1)S(1)}, u32[]{:S(2)}) copy-start(bf16[256,1024]{1,0:T(8,128)(2,1)S(1)} %gather_fusion.1) | copy-start | bytes 1572868
  136.1 101.3 %copy-start.75 = (f32[2,2,1024]{2,1,0:T(2,128)}, f32[2,2,1024]{2,1,0:T(2,128)S(1)}, u32[]{:S(2)}) copy-start(f32[2,2,1024]{2,1,0:T(2,128)S(1)} %reshape.455) | copy-start | bytes 49156
  136.6 100.7 %copy-start.80 = (f32[256]{0:T(256)}, f32[256]{0:T(256)S(1)}, u32[]{:S(2)}) copy-start(f32[256]{0:T(256)S(1)} %multiply_reduce_fusion.9) | copy-start | bytes 3076
  244.8 39.0 %copy-start.39 = (bf16[256,1024,1]{1,0,2:T(8,128)(2,1)}, bf16[256,1024,1]{1,0,2:T(8,128)(2,1)S(1)}, u32[]{:S(2)}) copy-start(bf16[256,1024,1]{1,0,2:T(8,128)(2,1)S(1)} %fusion.106) | copy-start | bytes 1572868
  287.0 98.3 %all-gather.22.cloned.1.call-start = ((), (), s32[]{:S(2)}) async-start(), calls=%async_computation.9 | async-start | bytes 2359296 | tf_op jit(solution)/shard_map/all_gather | solution.py:91
  287.6 192.7 %all-reduce.9.cloned.1.call-start = ((), (), s32[]{:S(2)}) async-start(), calls=%async_computation.10 | async-start | bytes 2097152 | tf_op jit(solution)/shard_map/psum | solution.py:49
  288.0 50.8 %copy-start.15 = (f32[1,256,512]{1,2,0:T(8,128)}, f32[1,256,512]{1,2,0:T(8,128)S(1)}, u32[]{:S(2)}) copy-start(f32[1,256,512]{1,2,0:T(8,128)S(1)} %copy.126) | copy-start | bytes 1572868
  441.5 38.7 %copy-start.4 = (bf16[256,1024]{1,0:T(8,128)(2,1)S(1)}, bf16[256,1024]{1,0:T(8,128)(2,1)}, u32[]{:S(2)}) copy-start(bf16[256,1024]{1,0:T(8,128)(2,1)} %copy-done.3) | copy-start | bytes 1572868
  441.5 38.7 %copy-start.7 = (bf16[256,1024]{1,0:T(8,128)(2,1)S(1)}, bf16[256,1024]{1,0:T(8,128)(2,1)}, u32[]{:S(2)}) copy-start(bf16[256,1024]{1,0:T(8,128)(2,1)} %copy-done.6) | copy-start | bytes 1572868
  441.6 116.7 %all-gather.24.cloned.1.call-start = ((), (), s32[]{:S(2)}) async-start(), calls=%async_computation.11 | async-start | bytes 8912896 | tf_op jit(solution)/shard_map/all_gather | solution.py:253
  442.5 163.6 %all-reduce.11.cloned.1.call-start = ((), (), s32[]{:S(2)}) async-start(), calls=%async_computation.12 | async-start | bytes 2097152 | tf_op jit(solution)/shard_map/psum | solution.py:49
  484.2 77.5 %copy-start.41 = (bf16[256,1024]{1,0:T(8,128)(2,1)}, bf16[256,1024]{1,0:T(8,128)(2,1)S(1)}, u32[]{:S(2)}) copy-start(bf16[256,1024]{1,0:T(8,128)(2,1)S(1)} %fusion.94) | copy-start | bytes 1572868
  567.7 33.1 %copy-start.88 = (s32[1,256]{1,0:T(1,128)S(1)}, s32[1,256]{1,0:T(1,128)}, u32[]{:S(2)}) copy-start(s32[1,256]{1,0:T(1,128)} %param.30) | copy-start | bytes 3076
  567.7 91.8 %all-gather.26.cloned.1.call-start = ((), (), s32[]{:S(2)}) async-start(), calls=%async_computation.13 | async-start | bytes 4456448 | tf_op jit(solution)/shard_map/all_gather | solution.py:254
  568.5 151.1 %all-reduce.13.cloned.1.call-start = ((), (), s32[]{:S(2)}) async-start(), calls=%async_computation.14 | async-start | bytes 2097152 | tf_op jit(solution)/shard_map/psum | solution.py:49
  607.9 113.6 %copy-start.1 = (f32[256,1024]{1,0:T(8,128)}, f32[256,1024]{1,0:T(8,128)S(1)}, u32[]{:S(2)}) copy-start(f32[256,1024]{1,0:T(8,128)S(1)} %get-tuple-element.484) | copy-start | bytes 3145732
  610.1 53.1 %copy-start.36 = (bf16[256,1024]{1,0:T(8,128)(2,1)}, bf16[256,1024]{1,0:T(8,128)(2,1)S(1)}, u32[]{:S(2)}) copy-start(bf16[256,1024]{1,0:T(8,128)(2,1)S(1)} %fusion.93) | copy-start | bytes 1572868
  659.5 18.9 copy-start.91
  663.2 15.2 copy-start.19
  680.9 93.0 %all-reduce.15.cloned.1.call-start = ((), (), s32[]{:S(2)}) async-start(), calls=%async_computation.15 | async-start | bytes 2097152 | tf_op jit(solution)/shard_map/psum | solution.py:49
  723.2 54.3 %copy-start.9 = (f32[256,1024]{1,0:T(8,128)}, f32[256,1024]{1,0:T(8,128)S(1)}, u32[]{:S(2)}) copy-start(f32[256,1024]{1,0:T(8,128)S(1)} %get-tuple-element.480) | copy-start | bytes 3145732
  723.2 8.2 slice-start.4
  725.5 5.9 slice-start.5
  733.7 339.0 %reduce-scatter.8.cloned.1.call-start = ((), (), s32[]{:S(2)}) async-start(), calls=%async_computation.16 | async-start | bytes 9437184 | tf_op jit(solution)/shard_map/reduce_scatter | solution.py:192
  923.5 197.0 %all-reduce.17.cloned.1.call-start = ((), (), s32[]{:S(2)}) async-start(), calls=%async_computation.17 | async-start | bytes 2097152 | tf_op jit(solution)/shard_map/psum | solution.py:49
  924.9 149.1 %copy-start.27 = (f32[1,256,512]{1,2,0:T(8,128)S(1)}, f32[1,256,512]{1,2,0:T(8,128)}, u32[]{:S(2)}) copy-start(f32[1,256,512]{1,2,0:T(8,128)} %copy-done.26) | copy-start | bytes 1572868
  1081.3 147.7 %reduce-scatter.14.cloned.1.call-start = ((), (), s32[]{:S(2)}) async-start(), calls=%async_computation.20 | async-start | bytes 8912896 | tf_op jit(solution)/shard_map/reduce_scatter | solution.py:327
  1087.5 315.4 %all-reduce.19.cloned.1.call-start = ((), (), s32[]{:S(2)}) async-start(), calls=%async_computation.22 | async-start | bytes 16777216
  1104.4 481.4 %reduce-scatter.12.cloned.1.call-start = ((), (), s32[]{:S(2)}) async-start(), calls=%async_computation.19 | async-start | bytes 17825792 | tf_op jit(solution)/shard_map/reduce_scatter | solution.py:326
  1115.0 5.5 copy-start.5
  1115.1 685.1 %reduce-scatter.16.cloned.1.call-start = ((), (), s32[]{:S(2)}) async-start(), calls=%async_computation.21 | async-start | bytes 22282240
  1115.7 6.9 copy-start.81
  1122.6 9.6 slice-start
  1124.7 7.6 slice-start.1
  1184.2 952.6 %reduce-scatter.10.cloned.1.call-start = ((), (), s32[]{:S(2)}) async-start(), calls=%async_computation.18 | async-start | bytes 35651584 | tf_op jit(solution)/shard_map/reduce_scatter | solution.py:324
  1803.2 380.1 %copy-start.78 = (f32[2,512]{1,0:T(2,128)S(1)}, f32[2,512]{1,0:T(2,128)}, u32[]{:S(2)}) copy-start(f32[2,512]{1,0:T(2,128)} %param.49) | copy-start | bytes 12292
  1803.2 380.1 %copy-start.82 = (f32[2,512]{1,0:T(2,128)S(1)}, f32[2,512]{1,0:T(2,128)}, u32[]{:S(2)}) copy-start(f32[2,512]{1,0:T(2,128)} %param.51) | copy-start | bytes 12292
  1803.2 380.1 %copy-start.83 = (f32[2,512]{1,0:T(2,128)S(1)}, f32[2,512]{1,0:T(2,128)}, u32[]{:S(2)}) copy-start(f32[2,512]{1,0:T(2,128)} %param.50) | copy-start | bytes 12292
  1803.2 380.7 %copy-start.44 = (f32[4,64,512]{2,1,0:T(8,128)S(1)}, f32[4,64,512]{2,1,0:T(8,128)}, u32[]{:S(2)}) copy-start(f32[4,64,512]{2,1,0:T(8,128)} %param.40) | copy-start | bytes 1572868
  1803.2 380.7 %copy-start.71 = (f32[4,64,512]{2,1,0:T(8,128)S(1)}, f32[4,64,512]{2,1,0:T(8,128)}, u32[]{:S(2)}) copy-start(f32[4,64,512]{2,1,0:T(8,128)} %param.42) | copy-start | bytes 1572868
  1803.2 380.7 %copy-start.72 = (f32[4,64,512]{2,1,0:T(8,128)S(1)}, f32[4,64,512]{2,1,0:T(8,128)}, u32[]{:S(2)}) copy-start(f32[4,64,512]{2,1,0:T(8,128)} %param.41) | copy-start | bytes 1572868
  2139.6 46.0 %copy-start.46 = (f32[64,2048]{1,0:T(8,128)S(1)}, f32[64,2048]{1,0:T(8,128)}, u32[]{:S(2)}) copy-start(f32[64,2048]{1,0:T(8,128)} %param.46) | copy-start | bytes 1572868
  2139.6 46.0 %copy-start.47 = (f32[64,2048]{1,0:T(8,128)S(1)}, f32[64,2048]{1,0:T(8,128)}, u32[]{:S(2)}) copy-start(f32[64,2048]{1,0:T(8,128)} %reduce-scatter.14.cloned.1.call-done) | copy-start | bytes 1572868
  (69 other events, 155.5 us)
Sparse Core Ops, SparseCore 0:
  10.9 90.5 all-gather.13
  104.2 125.0 all-gather.15
  232.1 48.7 all-gather.17
  287.1 47.7 all-gather.19
  337.4 47.7 all-gather.21
  441.7 38.5 all-reduce.8
  483.2 74.9 all-gather.23
  567.8 38.2 all-reduce.10
  608.9 50.5 all-gather.25
  681.0 38.5 all-reduce.12
  733.8 40.0 all-reduce.14
  923.7 149.0 reduce-scatter.7
  1081.4 39.0 all-reduce.16
  1124.4 104.5 reduce-scatter.13
  1232.6 170.2 all-reduce.18
  1407.4 178.3 reduce-scatter.11
  1590.3 209.8 reduce-scatter.15
  1804.9 331.8 reduce-scatter.9
where the time goes:
time: 2220 us; the launch traced here: 2210 us
  waiting for transfers between devices  1590 us (72%)
  matrix products  194 us (9%)
  local copies, waits for them, and re-layouts  127 us (6%)
  blocking collectives  119 us (5%)
  other arithmetic  104 us (5%)
  loops' own time  47.3 us (2%)
  between operations  24.8 us (1%)
    unnamed x20, waiting for transfers between devices  348 us
    reduce_scatter x1, waiting for transfers between devices, per_device(): lax.psum_scatter(grad_ada, ('seq', 'dp'), scatter_dimension=0, tiled=True)  330 us
    reduce_scatter x1, waiting for transfers between devices, per_device(): lax.psum_scatter(grad_mlp, ('seq', 'dp'), scatter_dimension=1, tiled=True)  181 us
    reduce_scatter x1, waiting for transfers between devices, layer_backward(): lax.psum_scatter(jnp.concatenate([joined_heads(part_keys), joined_heads(p...  147 us
    psum x5, waiting for transfers between devices, tp_total(): return lax.psum(value, 'tp')  127 us
    dot_general x56, matrix products, contract(): lax.dot_general(left, right, (((left_dim,), (right_dim,)), ((), ())), pre...  103 us
    all_gather x1, waiting for transfers between devices, per_device(): lax.all_gather(ada_w.astype(jnp.bfloat16), ('seq', 'dp'), axis=0, tiled=T...  92.7 us
    all_gather x1, waiting for transfers between devices, per_device(): lax.all_gather(tables_w.astype(jnp.bfloat16), ('seq', 'dp'), axis=1, tile...  89 us
  transfers between devices with their start and end apart: 18, of which 18 were waited for; matrix products, arithmetic and copies ran while one was open for 8% of the time, Pallas kernels for 0%

commit v1 on v0

v1 whole, which is shorter than its diff:
```python
import functools
import math

import jax
import jax.numpy as jnp
from jax import lax
from jax.experimental import pallas as pl
from jax.experimental.pallas import tpu as pltpu
from jax.sharding import PartitionSpec as P

HD = 64
V = 4096
NCLS = 1000
LEVELS = 10
STEP = 3
AXES = ("seq", "tp", "dp")
BLOCKED = -30000.0


def place(axes, sizes, index):
    coords = {axis: lax.axis_index(axis) for axis in AXES}
    for axis in reversed(axes):
        coords[axis] = lax.rem(index, sizes[axis])
        index = index // sizes[axis]
    return tuple(coords[axis] for axis in AXES)


def linear(axes, sizes):
    index = 0
    for axis in axes:
        index = index * sizes[axis] + lax.axis_index(axis)
    return index


def direct_kernel(axes, sizes, spreads, *refs):
    count = math.prod(sizes[axis] for axis in axes)
    number = len(spreads)
    sources, targets = refs[:number], refs[number : 2 * number]
    send, recv, own = refs[2 * number :]
    me = linear(axes, sizes)
    barrier = pltpu.get_barrier_semaphore()

    def peer_at(step):
        return lax.rem(me + step, count)

    def greet(step, carry):
        pl.semaphore_signal(
            barrier,
            inc=1,
            device_id=place(axes, sizes, peer_at(step)),
            device_id_type=pl.DeviceIdType.MESH,
        )
        return carry

    lax.fori_loop(1, count, greet, 0)
    pl.semaphore_wait(barrier, count - 1)

    def ends(index, peer):
        source = sources[index].at[peer] if spreads[index] else sources[index]
        return source, targets[index].at[me]

    def copy_at(step, index):
        peer = peer_at(step)
        source, target = ends(index, peer)
        return pltpu.make_async_remote_copy(
            src_ref=source,
            dst_ref=target,
            send_sem=send.at[index, step],
            recv_sem=recv.at[index, step],
            device_id=place(axes, sizes, peer),
            device_id_type=pl.DeviceIdType.MESH,
        )

    def start(step, carry):
        for index in range(number):
            copy_at(step, index).start()
        return carry

    def finish(step, carry):
        for index in range(number):
            copy_at(step, index).wait()
        return carry

    lax.fori_loop(1, count, start, 0)
    local = []
    for index in range(number):
        source, target = ends(index, me)
        local.append(pltpu.make_async_copy(source, target, own.at[index]))
        local[-1].start()
    lax.fori_loop(1, count, finish, 0)
    for copy in local:
        copy.wait()


def direct(payloads, axes, sizes, number):
    count = math.prod(sizes[axis] for axis in axes)
    values = [value for value, _ in payloads]
    spreads = tuple(spread for _, spread in payloads)
    shapes = [
        jax.ShapeDtypeStruct(value.shape if spread else (count,) + value.shape, value.dtype)
        for value, spread in payloads
    ]
    return pl.pallas_call(
        functools.partial(direct_kernel, axes, sizes, spreads),
        out_shape=shapes,
        in_specs=[pl.BlockSpec(memory_space=pl.ANY)] * len(values),
        out_specs=[pl.BlockSpec(memory_space=pl.ANY)] * len(values),
        scratch_shapes=[
            pltpu.SemaphoreType.DMA((len(values), count)),
            pltpu.SemaphoreType.DMA((len(values), count)),
            pltpu.SemaphoreType.DMA((len(values),)),
        ],
        compiler_params=pltpu.CompilerParams(collective_id=number, has_side_effects=True),
        name=f"direct_{number}",
    )(*values)


def pairs_kernel(sizes, heads, tokens, outward, count, *refs):
    sources, targets = refs[:count], refs[count : 2 * count]
    send, recv, own = refs[2 * count :]
    pairs = 2 * heads
    half = tokens // 2
    at_seq, at_tp, at_dp = (lax.axis_index(axis) for axis in AXES)
    base = at_seq // pairs * pairs
    me = lax.rem(at_seq, pairs)

    def device(peer):
        return (base + peer, at_tp, at_dp)

    barrier = pltpu.get_barrier_semaphore()
    for step in range(1, pairs):
        pl.semaphore_signal(
            barrier,
            inc=1,
            device_id=device(lax.rem(me + step, pairs)),
            device_id_type=pl.DeviceIdType.MESH,
        )
    pl.semaphore_wait(barrier, pairs - 1)

    def ends(index, piece, pair, chunk):
        row = lax.rem(pair // heads + at_dp, 2)
        inner = pl.ds(pl.multiple_of((row * 2 + piece) * half, half), half)
        outer = pl.ds(
            pl.multiple_of(chunk * tokens + lax.rem(piece + at_tp, 2) * half, half), half
        )
        head = lax.rem(pair, heads)
        if outward:
            return sources[index].at[:, head, :, inner], targets[index].at[:, :, outer]
        return sources[index].at[:, :, outer], targets[index].at[:, head, :, inner]

    copies = []
    for step in range(1, pairs):
        peer = lax.rem(me + step, pairs)
        pair, chunk = (peer, me) if outward else (me, peer)
        for index in range(count):
            for piece in range(2):
                source, target = ends(index, piece, pair, chunk)
                copies.append(
                    pltpu.make_async_remote_copy(
                        src_ref=source,
                        dst_ref=target,
                        send_sem=send.at[index, piece, step],
                        recv_sem=recv.at[index, piece, step],
                        device_id=device(peer),
                        device_id_type=pl.DeviceIdType.MESH,
                    )
                )
                copies[-1].start()
    for index in range(count):
        for piece in range(2):
            source, target = ends(index, piece, me, me)
            copies.append(pltpu.make_async_copy(source, target, own.at[index, piece]))
            copies[-1].start()
    for copy in copies:
        copy.wait()


def pair_exchange(values, sizes, heads, tokens, outward, number):
    pairs = 2 * heads
    if outward:
        shapes = [(v.shape[0], v.shape[2], pairs * tokens) for v in values]
    else:
        shapes = [(v.shape[0], heads, v.shape[1], 2 * tokens) for v in values]
    count = len(values)
    return pl.pallas_call(
        functools.partial(pairs_kernel, sizes, heads, tokens, outward, count),
        out_shape=[jax.ShapeDtypeStruct(s, v.dtype) for s, v in zip(shapes, values)],
        in_specs=[pl.BlockSpec(memory_space=pl.ANY)] * count,
        out_specs=[pl.BlockSpec(memory_space=pl.ANY)] * count,
        scratch_shapes=[
            pltpu.SemaphoreType.DMA((count, 2, pairs)),
            pltpu.SemaphoreType.DMA((count, 2, pairs)),
            pltpu.SemaphoreType.DMA((count, 2)),
        ],
        compiler_params=pltpu.CompilerParams(collective_id=number, has_side_effects=True),
        name=f"pairs_{number}",
    )(*values)


def swapped(value, axis):
    return lax.ppermute(value, axis, [(0, 1), (1, 0)])


def group_gather(value):
    row = jnp.concatenate([value, swapped(value, "tp")], 0)
    return jnp.concatenate([row, swapped(row, "dp")], 0)


def remote(source, target, send, recv, device):
    return pltpu.make_async_remote_copy(
        src_ref=source,
        dst_ref=target,
        send_sem=send,
        recv_sem=recv,
        device_id=device,
        device_id_type=pl.DeviceIdType.MESH,
    )


def reduce_steps(x, out, scratch, sizes):
    from_y, staged, from_low, from_high, b_staged, b_low, b_high, b_y, total, send, recv = scratch
    deep = sizes["seq"] // 2
    at_seq, at_tp, at_dp = (lax.axis_index(axis) for axis in AXES)
    z, y = at_seq // 2, lax.rem(at_seq, 2)
    beside = (at_seq + 1 - 2 * y, at_tp, at_dp)
    above = (lax.min(at_seq + 2, sizes["seq"] - 1), at_tp, at_dp)
    below = (lax.max(at_seq - 2, 0), at_tp, at_dp)
    split = from_y.shape[2]
    first, second = pl.ds(0, split), pl.ds(split, x.shape[3] - split)

    def block(index):
        return lax.rem(z + index, deep)

    def copy(kind, slot, source, target, device):
        return remote(source, target, send.at[kind, slot], recv.at[kind, slot], device)

    def y_copy(index):
        return copy(0, index, x.at[block(index), 1 - y, :, first], from_y.at[index], beside)

    def up_copy(turn):
        return copy(1, turn - 1, staged.at[deep - turn], from_low.at[turn - 1], above)

    def down_copy(turn):
        return copy(2, turn - 1, staged.at[turn], from_high.at[turn - 1], below)

    def b_up_copy(turn):
        return copy(3, turn - 1, b_staged.at[deep - turn], b_low.at[turn - 1], above)

    def b_down_copy(turn):
        return copy(4, turn - 1, b_staged.at[turn], b_high.at[turn - 1], below)

    def b_y_copy():
        return copy(5, 0, b_staged.at[0, 1 - y], b_y, beside)

    def goes_up(turn):
        return (z <= turn - 1) & (z < deep - 1)

    def goes_down(turn):
        return (z >= deep - turn) & (z > 0)

    def move(turn, went, index, there, arrived, received, started, b):
        @pl.when(went)
        def _():
            if b:
                b_staged[index] = x[block(index), :, :, second]
            else:
                y_copy(index).wait_recv()
                staged[index] = x[block(index), y, :, first] + from_y[index]
            if turn > 1:

                @pl.when(there)
                def _():
                    arrived(turn - 1).wait_recv()
                    if b:
                        b_staged[index] += received[turn - 2]
                    else:
                        staged[index] += received[turn - 2]

            started(turn).start()

    def main(turn):
        move(turn, goes_up(turn), deep - turn, z > 0, up_copy, from_low, up_copy, False)
        move(turn, goes_down(turn), turn, z < deep - 1, down_copy, from_high, down_copy, False)

    def rest(turn):
        move(turn, goes_up(turn), deep - turn, z > 0, b_up_copy, b_low, b_up_copy, True)
        move(turn, goes_down(turn), turn, z < deep - 1, b_down_copy, b_high, b_down_copy, True)

    def begin():
        for turn in range(deep - 1):
            y_copy(lax.select(z < deep // 2, deep - 1 - turn, turn + 1)).start()
        y_copy(0).start()
        rest(1)

    def rest_end():
        b_staged[0] = x[z, :, :, second]

        @pl.when(z > 0)
        def _():
            b_up_copy(deep - 1).wait_recv()
            b_staged[0] += b_low[deep - 2]

        @pl.when(z < deep - 1)
        def _():
            b_down_copy(deep - 1).wait_recv()
            b_staged[0] += b_high[deep - 2]

        b_y_copy().start()

    def middle(turn):
        main(turn)
        if turn < deep - 1:
            rest(turn + 1)
        else:
            rest_end()

    columns = x.shape[3]
    half = total.shape[0] // 2
    place_in = pl.ds(pl.multiple_of(at_dp * columns, 128), columns)

    def core_copy():
        given = total.at[pl.ds(pl.multiple_of((1 - at_dp) * half, half), half)]
        return copy(5, 1, given, out.at[:, place_in], (at_seq, at_tp, 1 - at_dp))

    def main_end():
        y_copy(0).wait_recv()
        total[:, first] = x[z, y, :, first] + from_y[0]

        @pl.when(z > 0)
        def _():
            up_copy(deep - 1).wait_recv()
            total[:, first] += from_low[deep - 2]

        @pl.when(z < deep - 1)
        def _():
            down_copy(deep - 1).wait_recv()
            total[:, first] += from_high[deep - 2]

    def finish():
        b_y_copy().wait_recv()
        total[:, second] = b_staged[0, y] + b_y[...]
        core_copy().start()
        out[:, place_in] = total[pl.ds(pl.multiple_of(at_dp * half, half), half), :]
        core_copy().wait()
        for index in range(deep):
            y_copy(index).wait_send()
        b_y_copy().wait_send()
        for turn in range(1, deep):

            @pl.when(goes_up(turn))
            def _():
                up_copy(turn).wait_send()
                b_up_copy(turn).wait_send()

            @pl.when(goes_down(turn))
            def _():
                down_copy(turn).wait_send()
                b_down_copy(turn).wait_send()

    turns = [functools.partial(middle, turn) for turn in range(1, deep)]
    return [begin] + turns + [main_end, finish]


def reduce_scratch(value):
    deep, _, rows, columns = value.shape
    split = max(128, columns * 3 // 4 // 128 * 128)
    rest = columns - split
    kind = value.dtype
    return [
        pltpu.VMEM((deep, rows, split), kind),
        pltpu.VMEM((deep, rows, split), kind),
        pltpu.VMEM((deep - 1, rows, split), kind),
        pltpu.VMEM((deep - 1, rows, split), kind),
        pltpu.VMEM((deep, 2, rows, rest), kind),
        pltpu.VMEM((deep - 1, 2, rows, rest), kind),
        pltpu.VMEM((deep - 1, 2, rows, rest), kind),
        pltpu.VMEM((rows, rest), kind),
        pltpu.VMEM((rows, columns), kind),
        pltpu.SemaphoreType.DMA((6, deep)),
        pltpu.SemaphoreType.DMA((6, deep)),
    ]


def reduced(value):
    rows, columns = value.shape[2:]
    return jax.ShapeDtypeStruct((rows // 2, 2 * columns), value.dtype)


def room(*shapes):
    size = 0
    for shape, kind in shapes:
        padded = list(shape)
        padded[-1] = -(-padded[-1] // 128) * 128
        if len(padded) > 1:
            padded[-2] = -(-padded[-2] // 16) * 16
        size += math.prod(padded) * jnp.dtype(kind).itemsize
    return min(size + 6 * 1024 * 1024, 60 * 1024 * 1024)


def sizes_of(scratch):
    return [(item.shape, item.dtype) for item in scratch if item.memory_space == pltpu.VMEM]


PIECES = 4


def normed_of(x):
    centered = x - jnp.mean(x, -1, keepdims=True)
    factor = lax.rsqrt(jnp.mean(centered * centered, -1, keepdims=True) + 1e-06)
    return centered * factor, factor


def stage_kernel(mode, parts, items, sizes, given, jobs, *refs):
    refs = list(refs)

    def take(count):
        taken, refs[:count] = refs[:count], []
        return taken

    terms, *values = take(given)
    mods, select = take(2)
    sums_in = take(jobs)
    gathers = mode != "last"
    first_out, second_out = take(2)
    gathered = take(1)[0] if gathers else None
    sums_out = take(jobs)
    from_core, passed, from_x, send, recv = take(5)
    scratch = [take(11) for _ in range(jobs)]
    block = terms.shape[1]
    size = block // PIECES
    at_seq, at_tp, at_dp = (lax.axis_index(axis) for axis in AXES)
    core, across = (at_seq, at_tp, 1 - at_dp), (at_seq, 1 - at_tp, at_dp)

    barrier = pltpu.get_barrier_semaphore()

    def greet(device):
        pl.semaphore_signal(barrier, inc=1, device_id=device, device_id_type=pl.DeviceIdType.MESH)

    greet(core)
    greet(across)
    expected = 2
    if jobs:
        z, y, deep = at_seq // 2, lax.rem(at_seq, 2), sizes["seq"] // 2
        greet((at_seq + 1 - 2 * y, at_tp, at_dp))

        @pl.when(z > 0)
        def _():
            greet((at_seq - 2, at_tp, at_dp))

        @pl.when(z < deep - 1)
        def _():
            greet((at_seq + 2, at_tp, at_dp))

        expected = 3 + lax.min(z, 1) + lax.min(deep - 1 - z, 1)
    pl.semaphore_wait(barrier, expected)

    def rows(piece):
        return pl.ds(piece * size, size)

    def copy(kind, piece, source, target, device):
        return remote(source, target, send.at[kind, piece], recv.at[kind, piece], device)

    def core_copy(piece):
        return copy(0, piece, terms.at[pl.ds(2, 2), rows(piece)], from_core.at[:, rows(piece)], core)

    def x_copy(piece):
        return copy(1, piece, passed.at[rows(piece)], from_x.at[rows(piece)], across)

    def share_x(piece):
        return copy(2, piece, gathered.at[0, rows(piece)], gathered.at[1, rows(piece)], across)

    def share_core(piece):
        return copy(3, piece, gathered.at[0, rows(piece)], gathered.at[2, rows(piece)], core)

    def forward_core(piece):
        return copy(4, piece, gathered.at[1, rows(piece)], gathered.at[3, rows(piece)], core)

    waiting = []
    for index in range(jobs):
        waiting.append(reduce_steps(sums_in[index], sums_out[index], scratch[index], sizes))

    def advance():
        for steps in waiting:
            if steps:
                steps.pop(0)()

    for piece in range(PIECES):
        core_copy(piece).start()
    advance()
    for piece in range(PIECES):
        at = rows(piece)
        core_copy(piece).wait_recv()
        passed[at, :] = terms[1, at, :] + from_core[1, at, :]
        x_copy(piece).start()
    for piece in range(PIECES):
        at = rows(piece)
        chosen = [select[at, i : i + 1] for i in range(items)]

        def mod(part):
            return sum(chosen[i] * mods[i * 8 + part : i * 8 + part + 1, :] for i in range(items))

        def tally(index, value):
            for i in range(items):
                slot = pl.ds(index * items + i, 1)
                part = jnp.sum(chosen[i] * value, 0, keepdims=True)
                if piece == 0:
                    second_out[slot, :] = part
                else:
                    second_out[slot, :] += part

        x_copy(piece).wait_recv()
        total = terms[0, at, :] + from_core[0, at, :] + from_x[at, :]
        if mode == "forward":
            gate, shift, scale = parts
            x = values[0][at, :] + mod(gate) * total
            first_out[at, :] = total
            second_out[at, :] = x
            result = normed_of(x)[0] * (1.0 + mod(scale)) + mod(shift)
        else:
            normed, factor = normed_of(values[0][at, :])
            grad = total * (1.0 + mod(parts[0]))
            d_x = factor * (
                grad
                - jnp.mean(grad, -1, keepdims=True)
                - normed * jnp.mean(grad * normed, -1, keepdims=True)
            )
            if given > (3 if gathers else 2):
                d_x = d_x + values[-1][at, :]
            first_out[at, :] = d_x
            tally(0, total)
            tally(1, total * normed)
            if gathers:
                tally(2, d_x * values[1][at, :])
                result = d_x * mod(parts[1])
        if gathers:
            gathered[0, at, :] = result.astype(jnp.bfloat16)
            share_x(piece).start()
            share_core(piece).start()
        advance()
    if gathers:
        for piece in range(PIECES):
            share_x(piece).wait_recv()
            forward_core(piece).start()
    while any(waiting):
        advance()
    for piece in range(PIECES):
        core_copy(piece).wait_send()
        x_copy(piece).wait_send()
        if gathers:
            share_core(piece).wait_recv()
            forward_core(piece).wait_recv()
            share_x(piece).wait_send()
            share_core(piece).wait_send()
            forward_core(piece).wait_send()


def stage(mode, parts, items, sizes, terms, values, mods, select, sums, number):
    block, width = terms.shape[0] // 4, terms.shape[1]
    f32, gathers = jnp.float32, mode != "last"
    inputs = [terms.reshape(4, block, width), *values, mods, select, *sums]
    second = {"forward": block, "backward": 3 * items, "last": 2 * items}[mode]
    shapes = [
        jax.ShapeDtypeStruct((block, width), f32),
        jax.ShapeDtypeStruct((second, width), f32),
    ]
    if gathers:
        shapes.append(jax.ShapeDtypeStruct((4, block, width), jnp.bfloat16))
    shapes += [reduced(value) for value in sums]
    scratch = [
        pltpu.VMEM((2, block, width), f32),
        pltpu.VMEM((block, width), f32),
        pltpu.VMEM((block, width), f32),
        pltpu.SemaphoreType.DMA((5, PIECES)),
        pltpu.SemaphoreType.DMA((5, PIECES)),
    ]
    for value in sums:
        scratch += reduce_scratch(value)
    results = pl.pallas_call(
        functools.partial(
            stage_kernel, mode, parts, items, sizes, 1 + len(values), len(sums)
        ),
        out_shape=shapes,
        in_specs=[pl.BlockSpec(memory_space=pltpu.VMEM)] * len(inputs),
        out_specs=[pl.BlockSpec(memory_space=pltpu.VMEM)] * len(shapes),
        scratch_shapes=scratch,
        compiler_params=pltpu.CompilerParams(
            collective_id=number,
            has_side_effects=True,
            vmem_limit_bytes=room(
                *((value.shape, value.dtype) for value in inputs + shapes), *sizes_of(scratch)
            ),
        ),
        name=f"stage_{number}",
    )(*inputs)
    outs = list(results)
    if gathers:
        outs[2] = outs[2].reshape(4 * block, width)
    return outs


def outer_kernel(dims, *refs):
    out = refs[-1]
    start = 0
    for index, dim in enumerate(dims):
        left, right = refs[2 * index], refs[2 * index + 1]
        count = right.shape[1 - dim] // 256

        def tile(step, carry, left=left, right=right, dim=dim, start=start):
            at = pl.ds(pl.multiple_of(step * 256, 256), 256)
            part = right[at, :] if dim else right[:, at]
            product = lax.dot_general(
                left[...], part, (((0,), (dim,)), ((), ())), preferred_element_type=jnp.float32
            )
            out[:, pl.ds(pl.multiple_of(start + step * 256, 256), 256)] = product.astype(out.dtype)
            return carry

        lax.fori_loop(0, count, tile, 0)
        start += count * 256


def outer(pairs, kind):
    dims = tuple(dim for _, _, dim in pairs)
    columns = sum(right.shape[1 - dim] for _, right, dim in pairs)
    inputs = [value for left, right, _ in pairs for value in (left, right)]
    rows, depth = pairs[0][0].shape[1], pairs[0][0].shape[0]
    return pl.pallas_call(
        functools.partial(outer_kernel, dims),
        out_shape=jax.ShapeDtypeStruct((rows, columns), kind),
        in_specs=[pl.BlockSpec(memory_space=pltpu.VMEM)] * len(inputs),
        out_specs=pl.BlockSpec(memory_space=pltpu.VMEM),
        cost_estimate=pl.CostEstimate(
            flops=2 * rows * columns * depth, bytes_accessed=8 * rows * columns, transcendentals=0
        ),
        compiler_params=pltpu.CompilerParams(
            vmem_limit_bytes=room(
                *((value.shape, value.dtype) for value in inputs), ((rows, columns), kind)
            )
        ),
        name="outer",
    )(*inputs)


def tail_kernel(items, sizes, *refs):
    cols, mods, x, own_codes, own_levels, other_codes, other_levels = refs[:7]
    mods_out, mods_in, sum_out, codes_out, levels_out = refs[7:12]
    own_cols, other_cols, parts, mods_own, mods_other, mods_sum = refs[12:18]
    send, recv, near, across_send, across_recv = refs[18:23]
    scratch = refs[23:]
    axes = ("seq", "dp")
    seq = sizes["seq"]
    count = seq * 2
    me = linear(axes, sizes)
    at_seq, at_tp, at_dp = (lax.axis_index(axis) for axis in AXES)
    across = (at_seq, 1 - at_tp, at_dp)
    barrier = pltpu.get_barrier_semaphore()

    def greet_device(device):
        pl.semaphore_signal(barrier, inc=1, device_id=device, device_id_type=pl.DeviceIdType.MESH)

    def greet(step, carry):
        greet_device(place(axes, sizes, lax.rem(me + step, count)))
        return carry

    lax.fori_loop(1, count, greet, 0)
    greet_device(across)
    pl.semaphore_wait(barrier, count)

    def ends(index, peer):
        if index == 0:
            return mods.at[peer], mods_in.at[me]
        if index == 1:
            return cols.at[peer], own_cols.at[me]
        return mods_sum, mods_out.at[me]

    def copy_at(index, step):
        peer = lax.rem(me + step, count)
        return remote(
            *ends(index, peer), send.at[index, step], recv.at[index, step], place(axes, sizes, peer)
        )

    def over_peers(index, action):
        def one(step, carry):
            getattr(copy_at(index, step), action)()
            return carry

        lax.fori_loop(1, count, one, 0)

    steps = reduce_steps(x, sum_out, scratch, sizes)

    def advance():
        if steps:
            steps.pop(0)()

    owners, width, block = own_cols.shape
    tokens = owners * block
    chunk = 1024
    tile = 512

    def fill(columns, side, owner):
        value = columns[owner]
        at = pl.ds(pl.multiple_of(owner * block, block), block)
        for index in range(3):
            part = value.astype(jnp.bfloat16)
            parts[side, pl.ds(index * width, width), at] = part
            value = value - part.astype(jnp.float32)

    def products(side, ids, first, height):
        def one(step, total):
            at = pl.ds(pl.multiple_of(step * chunk, chunk), chunk)
            rows = lax.broadcasted_iota(jnp.int32, (height, chunk), 0) + first
            hot = jnp.where(rows == ids[:, at], 1.0, 0.0).astype(jnp.bfloat16)
            return total + lax.dot_general(
                parts[side, :, at], hot, (((1,), (1,)), ((), ())), preferred_element_type=jnp.float32
            )

        total = jnp.zeros((3 * width, height), jnp.float32)
        total = lax.fori_loop(0, tokens // chunk, one, total)
        return total[:width] + total[width : 2 * width] + total[2 * width :]

    def tiles(side, codes, base, number):
        def one(step, carry):
            first = pl.multiple_of((base + step) * tile, tile)
            at = pl.ds(first, tile)
            value = products(side, codes, first, tile)
            if side:
                codes_out[:, at] += value
            else:
                codes_out[:, at] = value
            return carry

        lax.fori_loop(0, number, one, 0)

    def passed_on(owner):
        return remote(
            own_cols.at[owner],
            other_cols.at[owner],
            across_send.at[owner],
            across_recv.at[owner],
            across,
        )

    local = [pltpu.make_async_copy(*ends(index, me), near.at[index]) for index in range(3)]
    for index in range(2):
        over_peers(index, "start")
        local[index].start()
    over_peers(0, "wait")
    local[0].wait()
    for row in range(2):
        mine = mods_in[row, :items]
        for position in range(1, seq):
            mine = mine + mods_in[position * 2 + row, :items]
        mods_own[row] = mine
    mods_exchange = remote(
        mods_own, mods_other, across_send.at[owners], across_recv.at[owners], across
    )
    mods_exchange.start()
    local[1].wait()
    passed_on(me).start()
    fill(own_cols, 0, me)
    mods_exchange.wait()
    mods_sum[...] = mods_own[...] + mods_other[...]
    over_peers(2, "start")
    local[2].start()
    advance()

    def arrived(step, carry):
        copy_at(1, step).wait()
        owner = lax.rem(me - step + count, count)
        passed_on(owner).start()
        fill(own_cols, 0, owner)
        return carry

    lax.fori_loop(1, count, arrived, 0)
    advance()
    half = V // tile // 2
    tiles(0, own_codes, 0, half)
    advance()

    def crossed(owner, carry):
        passed_on(owner).wait()
        fill(other_cols, 1, owner)
        return carry

    lax.fori_loop(0, count, crossed, 0)
    tiles(0, own_codes, half, half)
    levels_out[...] = products(0, own_levels, 0, levels_out.shape[1])
    levels_out[...] += products(1, other_levels, 0, levels_out.shape[1])
    advance()
    tiles(1, other_codes, 0, half)
    advance()
    tiles(1, other_codes, half, half)
    while steps:
        advance()
    over_peers(2, "wait")
    local[2].wait()


def tail_stage(cols, mods, items, x, ids, sizes, number):
    count, width, block = cols.shape
    f32 = jnp.float32
    inputs = [cols, mods, x, *ids]
    in_vmem = pl.BlockSpec(memory_space=pltpu.VMEM)
    pair = (2, items, mods.shape[2])
    shapes = [
        jax.ShapeDtypeStruct((count,) + pair, f32),
        jax.ShapeDtypeStruct(mods.shape, f32),
        reduced(x),
        jax.ShapeDtypeStruct((width, V), f32),
        jax.ShapeDtypeStruct((width, 128), f32),
    ]
    scratch = [
        pltpu.VMEM(cols.shape, f32),
        pltpu.VMEM(cols.shape, f32),
        pltpu.VMEM((2, 3 * width, count * block), jnp.bfloat16),
        pltpu.VMEM(pair, f32),
        pltpu.VMEM(pair, f32),
        pltpu.VMEM(pair, f32),
        pltpu.SemaphoreType.DMA((3, count)),
        pltpu.SemaphoreType.DMA((3, count)),
        pltpu.SemaphoreType.DMA((3,)),
        pltpu.SemaphoreType.DMA((count + 1,)),
        pltpu.SemaphoreType.DMA((count + 1,)),
    ] + reduce_scratch(x)
    return pl.pallas_call(
        functools.partial(tail_kernel, items, sizes),
        out_shape=shapes,
        in_specs=[in_vmem] * len(inputs),
        out_specs=[in_vmem] * len(shapes),
        scratch_shapes=scratch,
        compiler_params=pltpu.CompilerParams(
            collective_id=number,
            has_side_effects=True,
            vmem_limit_bytes=room(
                *((value.shape, value.dtype) for value in inputs + shapes), *sizes_of(scratch)
            ),
        ),
        name=f"tail_{number}",
    )(*inputs)


def chunks(total):
    return min(total, 512)


def forward_kernel(
    limit_ref, q_ref, k_ref, v_ref, qg_ref, kg_ref, o_ref, inv_ref, qa_ref, ka_ref, exps
):
    step = pl.program_id(0)
    width = o_ref.shape[1]
    keys = k_ref.shape[1]
    size = chunks(keys)

    @pl.when(step == 0)
    def _():
        extra = ka_ref.shape[0] - HD
        ka_ref[:HD, :] = k_ref[...]
        level = lax.broadcasted_iota(jnp.int32, (extra, keys), 0)
        ka_ref[HD:, :] = jnp.where(level == kg_ref[...], 1.0, 0.0).astype(jnp.bfloat16)
        qa_ref[:HD, :] = q_ref[...]
        level = lax.broadcasted_iota(jnp.int32, (extra, q_ref.shape[1]), 0)
        open_ = (level <= qg_ref[0:1, :]) & (level >= qg_ref[1:2, :])
        qa_ref[HD:, :] = jnp.where(open_, 0.0, BLOCKED).astype(jnp.bfloat16)

    query = qa_ref[:, pl.ds(pl.multiple_of(step * width, 128), width)]

    def first(chunk, total):
        at = pl.ds(pl.multiple_of(chunk * size, 128), size)
        scores = lax.dot_general(
            ka_ref[:, at], query, (((0,), (0,)), ((), ())), preferred_element_type=jnp.float32
        )
        expd = jnp.exp(scores)
        exps[at, :] = expd
        return total + jnp.sum(expd, 0, keepdims=True)

    limit = limit_ref[step]
    total = lax.fori_loop(0, limit, first, jnp.zeros((1, width), jnp.float32))
    inverse = 1.0 / total
    inv_ref[...] = inverse

    def second(chunk, out):
        at = pl.ds(pl.multiple_of(chunk * size, 128), size)
        probs = (exps[at, :] * inverse).astype(jnp.bfloat16)
        return out + jnp.dot(v_ref[:, at], probs, preferred_element_type=jnp.float32)

    out = lax.fori_loop(0, limit, second, jnp.zeros((HD, width), jnp.float32))
    o_ref[...] = out.astype(jnp.bfloat16)


def query_width(keys):
    return 256 if keys <= 4096 else 128


def whole(shape):
    return pl.BlockSpec(shape, lambda step: (0,) * len(shape))


def kind_block(value, kind):
    return pl.BlockSpec((None,) + value.shape[1:], lambda step: (kind, 0, 0))


def attend_forward(own, everyone, query_groups, key_groups, extra, limits):
    queries, keys = own.shape[2], everyone.shape[2]
    width = query_width(keys)
    depth = HD + extra

    def part(rows):
        return pl.BlockSpec((rows, width), lambda step: (0, step))

    return pl.pallas_call(
        forward_kernel,
        grid=(queries // width,),
        out_shape=(
            jax.ShapeDtypeStruct((HD, queries), jnp.bfloat16),
            jax.ShapeDtypeStruct((1, queries), jnp.float32),
            jax.ShapeDtypeStruct((depth, queries), jnp.bfloat16),
            jax.ShapeDtypeStruct((depth, keys), jnp.bfloat16),
        ),
        in_specs=[
            pl.BlockSpec(memory_space=pltpu.SMEM),
            kind_block(own, 0),
            kind_block(everyone, 1),
            kind_block(everyone, 2),
            whole(query_groups.shape),
            whole(key_groups.shape),
        ],
        out_specs=(part(HD), part(1), whole((depth, queries)), whole((depth, keys))),
        scratch_shapes=[pltpu.VMEM((keys, width), jnp.float32)],
        compiler_params=pltpu.CompilerParams(
            vmem_limit_bytes=room(
                *(((depth, count), jnp.bfloat16) for count in (queries, keys) * 4),
                ((keys, width), jnp.float32),
                ((4 * HD, keys), jnp.float32),
            )
        ),
        name="attend_forward",
    )(limits, own, everyone, everyone, query_groups, key_groups)


def backward_kernel(
    limit_ref, qa_ref, ka_ref, v_ref, do_ref, inv_ref, dq_ref, dk_ref, dv_ref, probs_s, terms_s
):
    step = pl.program_id(0)
    width = dq_ref.shape[1]
    keys = v_ref.shape[1]
    size = chunks(keys)

    @pl.when(step == 0)
    def _():
        dk_ref[...] = jnp.zeros_like(dk_ref)
        dv_ref[...] = jnp.zeros_like(dv_ref)

    query = qa_ref[...]
    d_out = do_ref[...]
    inverse = inv_ref[...]

    def first(chunk, delta):
        at = pl.ds(pl.multiple_of(chunk * size, 128), size)
        scores = lax.dot_general(
            ka_ref[:, at], query, (((0,), (0,)), ((), ())), preferred_element_type=jnp.float32
        )
        probs = jnp.exp(scores) * inverse
        d_probs = lax.dot_general(
            v_ref[:, at], d_out, (((0,), (0,)), ((), ())), preferred_element_type=jnp.float32
        )
        terms = probs * d_probs
        probs_s[at, :] = probs
        terms_s[at, :] = terms
        return delta + jnp.sum(terms, 0, keepdims=True)

    limit = limit_ref[step]
    delta = lax.fori_loop(0, limit, first, jnp.zeros((1, width), jnp.float32))

    def second(chunk, d_query):
        at = pl.ds(pl.multiple_of(chunk * size, 128), size)
        probs = probs_s[at, :]
        d_scores = (terms_s[at, :] - probs * delta).astype(jnp.bfloat16)
        rows = (((1,), (1,)), ((), ()))
        dk_ref[:, at] += lax.dot_general(query[:HD], d_scores, rows, preferred_element_type=jnp.float32)
        dv_ref[:, at] += lax.dot_general(
            d_out, probs.astype(jnp.bfloat16), rows, preferred_element_type=jnp.float32
        )
        return d_query + jnp.dot(ka_ref[:HD, at], d_scores, preferred_element_type=jnp.float32)

    dq_ref[...] = lax.fori_loop(0, limit, second, jnp.zeros((HD, width), jnp.float32))


def attend_backward(qa, ka, everyone, d_out, inverse, limits):
    queries, keys = qa.shape[1], ka.shape[1]
    width = query_width(keys)

    def part(rows):
        return pl.BlockSpec((rows, width), lambda step: (0, step))

    return pl.pallas_call(
        backward_kernel,
        grid=(queries // width,),
        out_shape=(
            jax.ShapeDtypeStruct((HD, queries), jnp.float32),
            jax.ShapeDtypeStruct((HD, keys), jnp.float32),
            jax.ShapeDtypeStruct((HD, keys), jnp.float32),
        ),
        in_specs=[
            pl.BlockSpec(memory_space=pltpu.SMEM),
            part(qa.shape[0]),
            whole(ka.shape),
            kind_block(everyone, 2),
            part(HD),
            part(1),
        ],
        out_specs=(part(HD), whole((HD, keys)), whole((HD, keys))),
        scratch_shapes=[
            pltpu.VMEM((keys, width), jnp.float32),
            pltpu.VMEM((keys, width), jnp.float32),
        ],
        compiler_params=pltpu.CompilerParams(
            vmem_limit_bytes=room(
                *(((ka.shape[0], count), jnp.bfloat16) for count in (queries, keys) * 4),
                *(((keys, width), jnp.float32),) * 2,
                ((4 * HD, keys), jnp.float32),
            )
        ),
        name="attend_backward",
    )(limits, qa, ka, everyone, d_out, inverse)


def layer_mod(resid, shift, scale):
    centered = resid - jnp.mean(resid, -1, keepdims=True)
    normed = centered * lax.rsqrt(jnp.mean(centered * centered, -1, keepdims=True) + 1e-06)
    return normed * (1.0 + scale) + shift


def low(value):
    return lax.reduce_precision(value, 8, 7)


def norm_factor(value, axis):
    return lax.rsqrt(jnp.mean(value * value, axis, keepdims=True) + 1e-06)


def unit_back(grad, unit, factor):
    return factor * (grad - unit * jnp.mean(unit * grad, 0, keepdims=True))


def gelu_tanh(value):
    return jax.nn.gelu(value, approximate=True)


def contract(left, right, left_dim, right_dim):
    return lax.dot_general(
        left, right, (((left_dim,), (right_dim,)), ((), ())), preferred_element_type=jnp.float32
    )


def adamw(weight, first, second, grad, rate):
    first = 0.5 * first + 0.5 * grad
    second = 0.5 * second + 0.5 * grad * grad
    fix = 1.0 - 0.5**STEP
    update = first / fix / (jnp.sqrt(second / fix) + 1e-08)
    return (first, second, weight - rate * (update + 0.05 * weight))


def pick(value, index):
    return lax.dynamic_index_in_dim(value, index, 0, keepdims=False)


def per_device(
    codes,
    targets,
    tok_weights,
    group_ids,
    labels,
    tables_w,
    tables_m,
    tables_v,
    ada_w,
    ada_m,
    ada_v,
    attn_w,
    attn_m,
    attn_v,
    mlp_w,
    mlp_m,
    mlp_v,
    head_w,
    head_m,
    head_v,
    small_w,
    small_m,
    small_v,
):
    sizes = {axis: lax.axis_size(axis) for axis in AXES}
    seq = sizes["seq"]
    at_seq, at_tp, at_dp = (lax.axis_index(axis) for axis in AXES)
    bf16, f32 = jnp.bfloat16, jnp.float32
    tokens = codes.shape[1]
    block = tokens // 2
    width = ada_w.shape[1] // 8
    rows_own = tables_w.shape[1]
    owners = seq * 2
    rows, items = labels.shape
    quarter = head_w.shape[1] // 2
    head_cols = small_w.shape[1] // 2
    heads = head_cols // HD
    pairs = rows * heads

    def quarters(*weights):
        mine, other = [], []
        for value in weights:
            halves = value.astype(bf16).reshape(rows_own, 2, -1)
            mine.append(lax.dynamic_index_in_dim(halves, at_dp, 1, keepdims=False))
            other.append(lax.dynamic_index_in_dim(halves, 1 - at_dp, 1, keepdims=False))
        mine = jnp.concatenate(mine, 1)
        got = swapped(jnp.concatenate(other, 1), "dp")
        return jnp.where(
            at_dp == 0, jnp.concatenate([mine, got], 0), jnp.concatenate([got, mine], 0)
        )

    def everywhere(block):
        return lax.all_gather(block, "seq", axis=0, tiled=True)

    attn_block = quarters(attn_w[0], attn_w[1], attn_w[2], attn_w[3])
    codes, attn_block = lax.optimization_barrier((codes, attn_block))
    attn_all = everywhere(attn_block)
    w_qkv, w_out = jnp.split(attn_all, [3 * head_cols], 1)
    rest_block = quarters(mlp_w[0], mlp_w[1], head_w)
    codes, rest_block = lax.optimization_barrier((codes, rest_block))
    mlp_block, head_block = jnp.split(rest_block, [2 * quarter], 1)
    w_up, w_down = jnp.split(everywhere(mlp_block), 2, 1)
    w_head = everywhere(head_block)

    label_flat = labels.reshape(-1)
    class_ids = lax.broadcasted_iota(jnp.int32, (NCLS, 1), 0)
    classes = tables_w[V : V + NCLS].astype(bf16)
    cond_own = contract((class_ids == label_flat[None, :]).astype(bf16), classes, 0, 0)
    silu_own = low(jax.nn.silu(cond_own))
    ada = low(ada_w)
    mods_part = contract(silu_own.astype(bf16), ada.astype(bf16), 1, 0)
    mods_part = jnp.transpose(mods_part.reshape(rows * items, owners, -1), (1, 0, 2))

    groups_chunk = lax.dynamic_slice_in_dim(group_ids[0], at_seq * tokens, tokens)
    ints = jnp.stack([codes[0], targets[0], tok_weights[0], groups_chunk])
    levels = low(tables_w[V + NCLS :])
    slot = rows * items * (8 * width // owners)
    shared = [ints.astype(f32).reshape(-1), levels.reshape(-1)]
    extra = sum(value.size for value in shared)
    shared.append(jnp.zeros((-(slot + extra) % 1024,), f32))
    shared = jnp.broadcast_to(jnp.concatenate(shared)[None], (owners, (slot + extra + 1023) // 1024 * 1024 - slot))
    opening = jnp.concatenate([mods_part.reshape(owners, -1), shared], 1).reshape(owners, 8, -1)
    (opening,) = direct([(opening, True)], ("seq", "dp"), sizes, 1)
    opening = opening.reshape(owners, -1)
    mods_sum = opening[:, :slot].reshape(mods_part.shape)
    ints_all = opening[:, slot : slot + ints.size].astype(jnp.int32)
    levels = opening[:, slot + ints.size : slot + extra].reshape(owners, LEVELS, rows_own)
    levels = jnp.pad(levels.astype(bf16), ((0, 0), (0, 16 - LEVELS), (0, 0)))
    levels = jnp.transpose(levels, (1, 0, 2)).reshape(16, width)
    ints_all = ints_all.reshape(seq, rows, 4, tokens)
    own_ints = pick(ints_all, at_seq).reshape(rows, 4, 2, block)
    own_ints = jnp.where(at_dp == 0, own_ints, own_ints[::-1])
    own_ints = jnp.where(at_tp == 0, own_ints, own_ints[:, :, ::-1])
    own_ints = jnp.transpose(own_ints, (1, 0, 2, 3)).reshape(4, rows * tokens)
    weight_total = jnp.sum(ints_all[:, :, 2]).astype(f32)

    half_ints = ints_all.reshape(seq, rows, 4, 2, block)
    half_ints = lax.dynamic_index_in_dim(half_ints, at_tp, 3, keepdims=False)

    def one_hot(index, count):
        return (lax.broadcasted_iota(jnp.int32, (count, 1), 0) == index[None, :]).astype(bf16)

    looked = contract(tables_w[:V].astype(bf16), one_hot(half_ints[:, :, 0].reshape(-1), V), 0, 0).astype(bf16)
    looked = jnp.transpose(looked.reshape(rows_own, owners, block), (1, 0, 2))
    resid, mods_all = direct(
        [(looked, True), (jnp.sum(mods_sum, 0), False)], ("seq", "dp"), sizes, 2
    )
    level_of = own_ints[3, :block] % LEVELS
    resid = resid.reshape(width, block).T.astype(f32) + contract(one_hot(level_of, 16), levels, 0, 0)
    mods_all = jnp.transpose(mods_all, (1, 0, 2)).reshape(rows, items, 8, width)
    mods_own = pick(mods_all, at_dp)
    item_of = own_ints[3, :block] // LEVELS
    select = (item_of[:, None] == jnp.arange(items)[None, :]).astype(f32)

    def mod(part):
        return sum(select[:, i : i + 1] * mods_own[i, part][None, :] for i in range(items))

    mods_rows = mods_own.reshape(items * 8, width)
    select_lanes = jnp.pad(select, ((0, 0), (0, 128 - items)))

    def run_stage(mode, parts, terms, values, sums, number):
        return stage(
            mode, parts, items, sizes, terms, values, mods_rows, select_lanes, sums, number
        )

    both = ints_all.reshape(owners, 4, 2, block)
    both = jnp.where(at_tp == 0, both, both[:, :, ::-1])
    ids = [
        kind(both[:, index, side]).reshape(1, -1)
        for side in range(2)
        for index, kind in ((0, lambda value: value), (3, lambda value: value % LEVELS))
    ]
    h_one = group_gather(layer_mod(resid, mod(0), mod(1)).astype(bf16))
    qkv = contract(w_qkv, h_one, 0, 1).reshape(3, heads, HD, rows * tokens)
    bias = lax.dynamic_slice_in_dim(small_w, at_dp * head_cols, head_cols, 1)
    bias = bias.reshape(2, heads, HD, 1)
    q_raw, k_raw, v_raw = qkv[0] + bias[0], qkv[1], qkv[2] + bias[1]
    q_factor, k_factor = norm_factor(q_raw, 1), norm_factor(k_raw, 1)
    units = jnp.stack([q_raw * q_factor * 0.25, k_raw * k_factor, v_raw]).astype(bf16)
    factors = jnp.zeros((heads, 6, rows * tokens), f32)
    factors = jnp.concatenate([q_factor, k_factor, factors], 1)[None]
    pair_own, pair_factors = pair_exchange([units, factors], sizes, heads, tokens, True, 3)
    pair = at_seq % pairs
    row_groups = lax.dynamic_index_in_dim(ints_all[:, :, 3], pair // heads, 1, keepdims=False).reshape(1, -1)
    turns = seq // pairs
    same_pair = [[turn * pairs + index for turn in range(turns)] for index in range(pairs)]

    def own_keys(value):
        if turns == 1:
            return value
        return lax.psum_scatter(
            value, "seq", scatter_dimension=1, tiled=True, axis_index_groups=same_pair
        )

    pair_all = pair_own
    if turns > 1:
        pair_all = lax.all_gather(
            pair_own, "seq", axis=2, tiled=True, axis_index_groups=same_pair
        )
    query_groups = lax.dynamic_slice_in_dim(
        row_groups, at_seq // pairs * pairs * tokens, pairs * tokens, 1
    )
    query_groups = jnp.concatenate([query_groups, query_groups // LEVELS * LEVELS])
    extra = -(-items * LEVELS // 16) * 16
    key_levels = row_groups[0] % LEVELS
    top_levels = jnp.max((query_groups[0] % LEVELS).reshape(-1, query_width(seq * tokens)), 1)
    places = jnp.arange(1, seq * tokens + 1)
    reach = jnp.max(jnp.where(key_levels[None, :] <= top_levels[:, None], places[None, :], 0), 1)
    size = chunks(seq * tokens)
    limits = (reach + size - 1) // size
    out_pair, inverse, qa, ka = attend_forward(
        pair_own, pair_all, query_groups, row_groups, extra, limits
    )
    (heads_out,) = pair_exchange([out_pair[None]], sizes, heads, tokens, False, 4)
    heads_out = heads_out.reshape(head_cols, rows * tokens)
    attn_out, x_one, h_two = run_stage(
        "forward", (2, 3, 4), contract(heads_out, w_out, 0, 1), [resid], [], 10
    )
    up_val = contract(h_two, w_up, 1, 0)
    act = gelu_tanh(up_val).astype(bf16)
    mlp_out, x_two, h_three = run_stage(
        "forward", (5, 6, 7), contract(act, w_down, 1, 1), [x_one], [], 11
    )
    logits = contract(h_three, w_head, 1, 0)

    first_code = (at_tp * 2 + at_dp) * quarter
    hit = (own_ints[1][:, None] - first_code == jnp.arange(quarter)[None, :]).astype(f32)
    local_top = jnp.max(logits, 1)
    local_sum = jnp.sum(jnp.exp(logits - local_top[:, None]), 1)
    linear_part = 0.9 * jnp.sum(hit * logits, 1) + 0.1 / V * jnp.sum(logits, 1)
    stats = jnp.stack([local_top, local_sum, linear_part]).reshape(3, rows, 2, block)

    def stats_joined(one, two):
        top = jnp.maximum(one[0], two[0])
        total = one[1] * jnp.exp(one[0] - top) + two[1] * jnp.exp(two[0] - top)
        return jnp.stack([top, total, one[2] + two[2]])

    stats = stats_joined(stats, swapped(stats, "dp")[:, ::-1])
    stats = stats_joined(stats, swapped(stats, "tp")[:, :, ::-1])
    stats = stats.reshape(3, rows * tokens)
    log_total = stats[0] + jnp.log(stats[1])
    weights = own_ints[2].astype(f32)
    loss_part = jnp.sum((weights * (log_total - stats[2]))[:block])
    scale_rows = 128.0 * weights / weight_total
    probs = jnp.exp(logits - log_total[:, None])
    d_logits = (scale_rows[:, None] * (probs - 0.9 * hit - 0.1 / V)).astype(bf16)

    def scattered(value):
        return lax.psum_scatter(value, "seq", scatter_dimension=0, tiled=True).astype(f32)

    def by_place(value):
        return value.reshape(seq // 2, 2, 2 * rows_own, -1)

    d_h_three = contract(d_logits, w_head, 1, 1)
    cuts = [0, quarter * 4 // 8, quarter]
    head_parts = [
        by_place(contract(h_three, d_logits[:, first:last], 0, 0))
        for first, last in zip(cuts, cuts[1:])
    ]
    d_x_two, sums_three, d_mlp, grad_head_one = run_stage(
        "backward", (7, 5), d_h_three, [x_two, mlp_out], head_parts[:1], 12
    )
    d_act = contract(d_mlp, w_down, 1, 0)
    d_up = jax.vjp(gelu_tanh, up_val)[1](d_act)[0].astype(bf16)
    grad_mlp = outer([(h_two, d_up, 0), (d_mlp, act, 0)], bf16)
    grad_mlp, d_up = lax.optimization_barrier((grad_mlp, d_up))
    grad_mlp = scattered(grad_mlp)
    d_h_two = contract(d_up, w_up, 1, 1)
    d_x_one, sums_two, d_attn = run_stage(
        "backward", (4, 2), d_h_two, [x_one, attn_out, d_x_two], [], 13
    )
    d_heads = contract(w_out, d_attn, 0, 1).astype(bf16).reshape(1, heads, HD, rows * tokens)
    (d_out_pair,) = pair_exchange([d_heads], sizes, heads, tokens, True, 5)
    d_query, d_keys, d_values = attend_backward(qa, ka, pair_all, d_out_pair[0], inverse, limits)
    q_factor, k_factor = pair_factors[0, 0:1], pair_factors[0, 1:2]
    d_q = unit_back(d_query, pair_own[0].astype(f32) * 4.0, q_factor) * 0.25
    d_k = unit_back(own_keys(d_keys), pair_own[1].astype(f32), k_factor)
    stacked = jnp.stack([d_q, d_k, own_keys(d_values)]).astype(bf16)
    (d_qkv,) = pair_exchange([stacked], sizes, heads, tokens, False, 6)
    d_qkv = d_qkv.reshape(3 * head_cols, rows * tokens)
    grad_attn = outer([(h_one, d_qkv, 1), (d_attn, heads_out, 1)], f32)
    bias_sums = jnp.sum(d_qkv.astype(f32), 1).reshape(3, head_cols)[::2]
    d_resid, sums_one, grad_head_two = run_stage(
        "last",
        (1,),
        contract(d_qkv, w_qkv, 0, 1),
        [resid, d_x_one],
        head_parts[1:],
        14,
    )

    gate = 2 * items
    d_mods = jnp.concatenate(
        [sums_one, sums_two[gate:], sums_two[:gate], sums_three[gate:], sums_three[:gate]], 0
    )
    d_mods = d_mods.reshape(8, items, owners // 8, -1)
    d_mods = jnp.transpose(d_mods, (0, 2, 1, 3)).reshape(owners, items, -1)
    d_cols = d_resid.T.reshape(owners, rows_own, block)
    slot = d_mods.shape[2]
    bias_row = jnp.pad(bias_sums.reshape(-1), (0, -bias_sums.size % slot)).reshape(-1, slot)
    d_mods = jnp.concatenate([d_mods, jnp.broadcast_to(bias_row, (owners,) + bias_row.shape)], 1)
    d_mods, d_mods_in, grad_attn, g_codes, g_levels = tail_stage(
        d_cols, d_mods, items, by_place(grad_attn), ids, sizes, 8
    )
    bias_sums = d_mods_in[:, items:].reshape(owners, -1)[:, : 2 * head_cols]
    bias_sums = jnp.sum(bias_sums.reshape(seq, 2, 2, head_cols), 0)
    g_small = jnp.concatenate([bias_sums[0], bias_sums[1]], 1)
    d_mods = d_mods.reshape(owners, rows * items, -1)
    d_mods = jnp.transpose(d_mods, (1, 0, 2)).reshape(rows * items, 8 * width)
    g_ada = sum(silu_own[i][:, None] * d_mods[i][None, :] for i in range(rows * items))
    d_silu = jnp.stack([jnp.sum(ada * d_mods[i][None, :], 1) for i in range(rows * items)])
    d_cond = jax.vjp(jax.nn.silu, cond_own)[1](d_silu)[0]

    class_lanes = lax.broadcasted_iota(jnp.int32, (1, NCLS), 1)
    g_classes = sum(
        jnp.where(class_lanes == label_flat[i], d_cond[i][:, None], 0.0) for i in range(rows * items)
    )
    g_tables = jnp.concatenate([g_codes, g_classes, g_levels[:, :LEVELS]], 1).T

    def owned(value):
        parts = value.reshape(2, rows_own, -1)
        mine = pick(parts, at_dp)
        return mine, swapped(pick(parts, 1 - at_dp), "dp")

    def joined(pair, first, count):
        mine, got = (part[:, first : first + count] for part in pair)
        return jnp.where(
            at_dp == 0, jnp.concatenate([mine, got], 1), jnp.concatenate([got, mine], 1)
        )

    def side_by_side(value, first, count):
        other = value.shape[1] // 2 + first
        return [value[:, first : first + count], value[:, other : other + count]]

    g_attn = jnp.stack(
        [
            jnp.concatenate(side_by_side(grad_attn, kind * head_cols, head_cols), 1)
            for kind in range(4)
        ]
    )
    mlp_pair = owned(grad_mlp)
    g_mlp = jnp.stack([joined(mlp_pair, kind * quarter, quarter) for kind in range(2)])
    one, two = (
        side_by_side(value, 0, value.shape[1] // 2) for value in (grad_head_one, grad_head_two)
    )
    g_head = jnp.concatenate([one[0], two[0], one[1], two[1]], 1)

    local_squares = (jnp.sum(g_tables * g_tables) + jnp.sum(g_ada * g_ada)) / 2
    local_squares = (
        local_squares
        + sum(
            jnp.sum(value * value)
            for value in (grad_attn, grad_mlp, grad_head_one, grad_head_two)
        )
    )
    local_squares = local_squares + jnp.sum(g_small * g_small) / owners
    column = lax.broadcasted_iota(jnp.int32, (8, 128), 1)
    scalars = jnp.where(column == 0, local_squares, jnp.where(column == 1, loss_part, 0.0))
    scalars = jnp.sum(direct([(scalars, False)], AXES, sizes, 9)[0], 0)
    grad_norm = jnp.sqrt(scalars[0, 0])
    loss = 128.0 * scalars[0, 1] / weight_total
    factor = jnp.minimum(1.0, 1.0 / (grad_norm + 1e-06))
    tables_n = adamw(tables_w, tables_m, tables_v, g_tables * factor, 0.3)
    ada_n = adamw(ada_w, ada_m, ada_v, g_ada * factor, 0.03)
    attn_n = adamw(attn_w, attn_m, attn_v, g_attn * factor, 0.1)
    mlp_n = adamw(mlp_w, mlp_m, mlp_v, g_mlp * factor, 0.02)
    head_n = adamw(head_w, head_m, head_v, g_head * factor, 0.03)
    small_n = adamw(small_w, small_m, small_v, g_small * factor, 0.5)
    return (
        loss,
        grad_norm,
        *tables_n,
        *ada_n,
        *attn_n,
        attn_n[2].astype(bf16),
        *mlp_n,
        mlp_n[2].astype(bf16),
        *head_n,
        head_n[2].astype(bf16),
        *small_n,
    )


def solution(mesh):
    tokens, whole_rows = P("dp", "seq"), P("dp", None)
    tables, ada = P(None, ("seq", "dp")), P(("seq", "dp"), None)
    layer, head, small = P(None, ("seq", "dp"), "tp"), P(("seq", "dp"), "tp"), P(None, "tp")
    return jax.shard_map(
        per_device,
        mesh=mesh,
        in_specs=(
            (tokens,) * 3
            + (whole_rows, P())
            + (tables,) * 3
            + (ada,) * 3
            + (layer,) * 6
            + (head,) * 3
            + (small,) * 3
        ),
        out_specs=(
            (P(), P())
            + (tables,) * 3
            + (ada,) * 3
            + (layer,) * 8
            + (head,) * 4
            + (small,) * 3
        ),
        check_vma=False,
    )
```

time: 2220 us -> 549 us (0.25)
  waiting for transfers between devices: 1590 us -> 18.4 us
  Pallas kernels: 0 us -> 368 us
  matrix products: 194 us -> 33.6 us
  blocking collectives: 119 us -> 0 us
  local copies, waits for them, and re-layouts: 127 us -> 44.9 us
  other arithmetic: 104 us -> 49.3 us
  loops' own time: 47.3 us -> 0 us
    reduce_scatter x4 -> x1, waiting for transfers between devices: 684 us -> 0.02 us  [scattered(): lax.psum_scatter(value, 'seq', scatter_dimension=0, tiled=True).astype(f32)]
    all_gather x7 -> x3, waiting for transfers between devices: 434 us -> 10.3 us  [everywhere(): return lax.all_gather(block, 'seq', axis=0, tiled=True)]
    pallas_call x0 -> x17, Pallas kernels: none -> 368 us  [the longest x5 137 us: stage(): pl.pallas_call(functools.partial(stage_kernel, mode, parts, items, sizes,...]
    unnamed x20 -> x4, waiting for transfers between devices: 348 us -> 0.07 us
    psum x5 -> x0, waiting for transfers between devices: 127 us -> none  [tp_total(): return lax.psum(value, 'tp')]
    psum x3 -> x0, blocking collectives: 106 us -> none  [the longest x2 66.7 us: per_device(): lax.psum((jnp.sum(weights * token_loss), jnp.sum(weights)), ('seq', 'dp'))]
    dot_general x28 -> x0, matrix products: 91 us -> none  [the longest x1 17.3 us: per_device(): lax.dot_general(silu_own.astype(jnp.float32), d_mods_items, (((0,), (0,))...]
    dot_general x56 -> x16, matrix products: 103 us -> 33.6 us  [contract(): lax.dot_general(left, right, (((left_dim,), (right_dim,)), ((), ())), pre...]
  transfers between devices with their start and end apart: 18 -> 11, of which waited for: 18 -> 6; matrix products, arithmetic and copies ran while one was open for 8% -> 16% of each run, Pallas kernels for 0% -> 59%
where the time goes in v1:
time: 549 us; the launch traced here: 544 us
  Pallas kernels  368 us (67%)
  other arithmetic  49.3 us (9%)
  local copies, waits for them, and re-layouts  44.9 us (8%)
  matrix products  33.6 us (6%)
  between operations  24.8 us (5%)
  waiting for transfers between devices  18.4 us (3%)
    pallas_call x5, Pallas kernels, stage(): pl.pallas_call(functools.partial(stage_kernel, mode, parts, items, sizes,...  137 us
    pallas_call x4, Pallas kernels, pair_exchange(): pl.pallas_call(functools.partial(pairs_kernel, sizes, heads, tokens, outw...  86.6 us
    pallas_call x1, Pallas kernels, tail_stage(): pl.pallas_call(functools.partial(tail_kernel, items, sizes), out_shape=sh...  64.7 us
    pallas_call x3, Pallas kernels, direct(): pl.pallas_call(functools.partial(direct_kernel, axes, sizes, spreads), ou...  41.8 us
    dot_general x16, matrix products, contract(): lax.dot_general(left, right, (((left_dim,), (right_dim,)), ((), ())), pre...  33.6 us
    unnamed x218, local copies, waits for them, and re-layouts  21.8 us
    pallas_call x1, Pallas kernels, attend_backward(): pl.pallas_call(backward_kernel, grid=(queries // width,), out_shape=(jax....  18.1 us
    pallas_call x1, Pallas kernels, attend_forward(): pl.pallas_call(forward_kernel, grid=(queries // width,), out_shape=(jax.S...  13 us
  transfers between devices with their start and end apart: 11, of which 6 were waited for; matrix products, arithmetic and copies ran while one was open for 16% of the time, Pallas kernels for 59%

profile of v1, /device:TPU:0, one launch (start us, length us, event | category | flops | bytes accessed | tf_op | source)
XLA Modules:
  0.0 543.9 jit_solution(4499325439179298842)
XLA Ops:
  20.5 1.9 iota_compare_fusion.11
  22.3 1.9 iota_compare_fusion.13
  27.1 11.6 %direct_1.1 = f32[16,8,512]{2,1,0:T(8,128)} custom-call(f32[16,8,512]{2,1,0:T(8,128)} %pad_maximum_fusion.5.refs_0_), custom_call_target="tpu_custom_call" | custom-call | tf_op jit(solution)/shard_map/direct_1/pallas_call | solution.py:103
  40.3 5.7 %fusion.28 = bf16[8,16,8,128]{3,2,1,0:T(8,128)(2,1)S(1)} fusion(s32[2048]{0:T(1024)S(1)} %bitcast.363, bf16[5106,64]{0,1:T(8,128)(2,1)S(1)} %copy-done.59), kind=kOutput, calls=%fused_computation.53 | convolution fusion | flops 1082261504 | bytes 794624 | tf_op jit(solution)/shard_map/dot_general | solution.py:1049
  47.4 16.7 %direct_2.1 = (bf16[16,64,128]{2,1,0:T(8,128)(2,1)}, f32[16,4,512]{2,1,0:T(4,128)}) custom-call(bf16[16,64,128]{2,1,0:T(8,128)(2,1)} %bitcast.302, f32[4,512]{1,0:T(4,128)} %reduce_sum.237.refs_1_), custom_call_target="tpu_custom_call" | custom-call | tf_op jit(solution)/shard_map/direct_2/pallas_call | solution.py:103
  67.8 1.7 collective-permute-start.2
  70.4 1.7 split.23
  72.2 3.8 collective-permute-done.2
  76.4 1.6 collective-permute-done.3
  78.1 2.6 fusion.25
  83.0 31.3 %pairs_3.1 = (bf16[3,64,2048]{2,1,0:T(8,128)(2,1)}, f32[1,8,2048]{2,1,0:T(8,128)}) custom-call(bf16[3,4,64,512]{3,2,1,0:T(8,128)(2,1)} %pad_maximum_fusion.1.refs_0_, f32[1,4,8,512]{3,2,1,0:T(8,128)} %maximum_bitcast_fusion.4.refs_1_), custom_call_target="tpu_custom_call" | custom-call | tf_op jit(solution)/shard_map/pairs_3/pallas_call | solution.py:185
  115.4 13.0 %attend_forward.1 = (bf16[64,2048]{1,0:T(8,128)(2,1)S(1)}, f32[1,2048]{1,0:T(1,128)S(1)}, bf16[96,2048]{1,0:T(8,128)(2,1)S(1)}, bf16[96,2048]{1,0:T(8,128)(2,1)S(1)}) custom-call(s32[8]{0:T(128)S(1)} %and_select_fusion.3.limit_ref, bf16[3,64,2048]{2,1,0:T(8,128)(2,1)S(1)} %copy-done.2, bf16[3,64,2048]{2,1,0:T(8,128)(2,1)S(1)} %copy-done.2, ...), custom_call_target="tpu_custom_call" | custom-call | tf_op jit(solution)/shard_map/attend_forward/pallas_call | solution.py:909
  129.2 17.8 %pairs_4.1 = bf16[1,4,64,512]{3,2,1,0:T(8,128)(2,1)} custom-call(bf16[1,64,2048]{2,1,0:T(8,128)(2,1)} %bitcast.291), custom_call_target="tpu_custom_call" | custom-call | tf_op jit(solution)/shard_map/pairs_4/pallas_call | solution.py:185
  148.0 1.6 fusion.46.refs_0_
  149.6 22.6 %stage_10.1 = (f32[128,1024]{1,0:T(8,128)S(1)}, f32[128,1024]{1,0:T(8,128)S(1)}, bf16[4,128,1024]{2,1,0:T(8,128)(2,1)S(1)}) custom-call(f32[4,128,1024]{2,1,0:T(8,128)S(1)} %fusion.46.refs_0_, f32[128,1024]{1,0:T(8,128)S(1)} %get-tuple-element.230.refs_1_, f32[16,1024]{1,0:T(8,128)S(1)} %get-tuple-element.177.refs_2_.refs_3_.refs_4_, ...), custom_call_target="tpu_custom_call" | custom-call | tf_op jit(solution)/shard_map/stage_10/pallas_call | solution.py:578
  173.0 4.9 multiply_convert_fusion.1
  179.2 22.6 %stage_11.1 = (f32[128,1024]{1,0:T(8,128)S(1)}, f32[128,1024]{1,0:T(8,128)S(1)}, bf16[4,128,1024]{2,1,0:T(8,128)(2,1)S(1)}) custom-call(f32[4,128,1024]{2,1,0:T(8,128)S(1)} %bitcast.279, f32[128,1024]{1,0:T(8,128)S(1)} %get-tuple-element.73.refs_1_, f32[16,1024]{1,0:T(8,128)S(1)} %get-tuple-element.177.refs_2_.refs_3_.refs_4_, ...), custom_call_target="tpu_custom_call" | custom-call | tf_op jit(solution)/shard_map/stage_11/pallas_call | solution.py:578
  203.3 10.3 %all-gather.8.cloned.1.call-done = bf16[1024,1024]{1,0:T(8,128)(2,1)} async-done(((bf16[128,1024]{1,0:T(8,128)(2,1)}), bf16[1024,1024]{1,0:T(8,128)(2,1)}) %all-gather.8.cloned.1.call-update) | async-done | bytes 2097168 | tf_op jit(solution)/shard_map/all_gather | solution.py:1119
  213.6 2.9 fusion.97
  216.6 1.3 copy-done.38
  220.0 1.5 collective-permute-start.5
  222.8 1.3 copy.133
  224.8 2.3 multiply_convert_fusion
  230.5 29.5 %stage_12.1 = (f32[128,1024]{1,0:T(8,128)S(1)}, f32[6,1024]{1,0:T(8,128)S(1)}, bf16[4,128,1024]{2,1,0:T(8,128)(2,1)S(1)}, f32[64,1024]{1,0:T(8,128)S(1)}) custom-call(f32[4,128,1024]{2,1,0:T(8,128)S(1)} %bitcast.280, f32[128,1024]{1,0:T(8,128)S(1)} %copy-done.22, f32[128,1024]{1,0:T(8,128)S(1)} %copy-done.20, ...), custom_call_target="tpu_custom_call" | custom-call | tf_op jit(solution)/shard_map/stage_12/pallas_call | solution.py:578
  260.0 2.3 fusion.9.refs_1_
  262.4 4.2 outer.2
  266.6 2.0 copy-done.4
  273.0 1.5 fusion.90
  274.5 3.0 fusion.16
  277.5 22.6 %stage_13.1 = (f32[128,1024]{1,0:T(8,128)S(1)}, f32[6,1024]{1,0:T(8,128)S(1)}, bf16[4,128,1024]{2,1,0:T(8,128)(2,1)S(1)}) custom-call(f32[4,128,1024]{2,1,0:T(8,128)S(1)} %bitcast.278, f32[128,1024]{1,0:T(8,128)S(1)} %get-tuple-element.73.refs_1_, f32[128,1024]{1,0:T(8,128)S(1)} %copy-done.18, f32[128,1024]{1,0:T(8,128)S(1)} %copy-done.26, ...), custom_call_target="tpu_custom_call" | custom-call | tf_op jit(solution)/shard_map/stage_13/pallas_call | solution.py:578
  302.5 2.3 convolution_convert_fusion
  305.8 11.4 %pairs_5.1 = bf16[1,64,2048]{2,1,0:T(8,128)(2,1)} custom-call(bf16[1,4,64,512]{3,2,1,0:T(8,128)(2,1)} %bitcast.328), custom_call_target="tpu_custom_call" | custom-call | tf_op jit(solution)/shard_map/pairs_5/pallas_call | solution.py:185
  318.8 18.1 %attend_backward.1 = (f32[64,2048]{1,0:T(8,128)S(1)}, f32[64,2048]{1,0:T(8,128)S(1)}, f32[64,2048]{1,0:T(8,128)S(1)}) custom-call(s32[8]{0:T(128)S(1)} %copy-done.34, bf16[96,2048]{1,0:T(8,128)(2,1)S(1)} %get-tuple-element.68.qa_ref, bf16[96,2048]{1,0:T(8,128)(2,1)S(1)} %get-tuple-element.69.ka_ref, bf16[3,64,2048]{2,1,0:T(8,128)(2,1)S(1)} %copy-done.3, ...), custom_call_target="tpu_custom_call" | custom-call | tf_op jit(solution)/shard_map/attend_backward/pallas_call | solution.py:994
  338.4 26.1 %pairs_6.1 = bf16[3,4,64,512]{3,2,1,0:T(8,128)(2,1)} custom-call(bf16[3,64,2048]{2,1,0:T(8,128)(2,1)} %pad_maximum_fusion.2.refs_0_), custom_call_target="tpu_custom_call" | custom-call | tf_op jit(solution)/shard_map/pairs_6/pallas_call | solution.py:185
  364.5 1.4 copy.140
  365.9 2.2 fusion.43.refs_5_
  369.3 40.2 %stage_14.1 = (f32[128,1024]{1,0:T(8,128)S(1)}, f32[4,1024]{1,0:T(4,128)S(1)}, f32[64,1024]{1,0:T(8,128)S(1)}) custom-call(f32[4,128,1024]{2,1,0:T(8,128)S(1)} %fusion.20.refs_0_, f32[128,1024]{1,0:T(8,128)S(1)} %get-tuple-element.230.refs_1_, f32[128,1024]{1,0:T(8,128)S(1)} %copy-done.24, f32[16,1024]{1,0:T(8,128)S(1)} %get-tuple-element.177.refs_2_.refs_3_.refs_4_, ...), custom_call_target="tpu_custom_call" | custom-call | tf_op jit(solution)/shard_map/stage_14/pallas_call | solution.py:578
  413.4 2.0 outer.3
  415.6 64.7 %tail_8.1 = (f32[16,2,2,512]{3,2,1,0:T(2,128)S(1)}, f32[16,3,512]{2,1,0:T(4,128)S(1)}, f32[64,2048]{1,0:T(8,128)S(1)}, f32[64,4096]{1,0:T(8,128)S(1)}, f32[64,128]{1,0:T(8,128)S(1)}) custom-call(f32[16,64,128]{2,1,0:T(8,128)S(1)} %bitcast.277, f32[16,3,512]{2,1,0:T(4,128)S(1)} %pad_maximum_fusion.7.refs_1_, f32[4,2,128,1024]{3,2,1,0:T(8,128)S(1)} %bitcast.272, ...), custom_call_target="tpu_custom_call" | custom-call | tf_op jit(solution)/shard_map/tail_8/pallas_call | solution.py:824
  480.8 3.6 multiply_reduce_fusion.4
  494.2 1.9 multiply_reduce_fusion.6
  499.3 13.5 %direct_9.1 = f32[32,8,128]{2,1,0:T(8,128)} custom-call(f32[8,128]{1,0:T(8,128)} %broadcast_select_fusion.1.refs_0_), custom_call_target="tpu_custom_call" | custom-call | tf_op jit(solution)/shard_map/direct_9/pallas_call | solution.py:103
  515.8 1.3 convert.99
  518.1 2.7 multiply_subtract_fusion.1
  522.4 4.4 multiply_subtract_fusion
  527.5 1.5 fusion.79
  529.1 1.5 fusion.75
  532.5 2.5 fusion.77
  (412 shorter events, 69.9 us)
Async XLA Ops:
  7.2 12.7 %copy-start = (s32[1,2048]{1,0:T(1,128)S(1)}, s32[1,2048]{1,0:T(1,128)}, u32[]{:S(2)}) copy-start(s32[1,2048]{1,0:T(1,128)} %param.26) | copy-start | bytes 24580
  7.2 70.8 %all-gather.4.cloned.1.call-start = ((), (), s32[]{:S(2)}) async-start(), calls=%async_computation.1 | async-start | bytes 2359296 | tf_op jit(solution)/shard_map/all_gather | solution.py:1119
  9.2 1.5 collective-permute-start
  11.4 161.5 %all-gather.6.cloned.1.call-start = ((), (), s32[]{:S(2)}) async-start(), calls=%async_computation.2 | async-start | bytes 4718592 | tf_op jit(solution)/shard_map/all_gather | solution.py:1119
  14.1 1.8 collective-permute-start.1
  16.9 9.1 %copy-start.35 = (f32[64,8192]{1,0:T(8,128)S(1)}, f32[64,8192]{1,0:T(8,128)}, u32[]{:S(2)}) copy-start(f32[64,8192]{1,0:T(8,128)} %param.31) | copy-start | bytes 6291460
  17.8 195.9 %all-gather.8.cloned.1.call-start = ((), (), s32[]{:S(2)}) async-start(), calls=%async_computation.3 | async-start | bytes 2359296 | tf_op jit(solution)/shard_map/all_gather | solution.py:1119
  18.4 7.9 %copy-start.91 = (s32[1,256]{1,0:T(1,128)S(1)}, s32[1,256]{1,0:T(1,128)}, u32[]{:S(2)}) copy-start(s32[1,256]{1,0:T(1,128)} %param.25) | copy-start | bytes 3076
  18.4 7.9 %copy-start.92 = (s32[1,256]{1,0:T(1,128)S(1)}, s32[1,256]{1,0:T(1,128)}, u32[]{:S(2)}) copy-start(s32[1,256]{1,0:T(1,128)} %param.24) | copy-start | bytes 3076
  18.4 7.9 %copy-start.93 = (s32[1,256]{1,0:T(1,128)S(1)}, s32[1,256]{1,0:T(1,128)}, u32[]{:S(2)}) copy-start(s32[1,256]{1,0:T(1,128)} %param.23) | copy-start | bytes 3076
  26.0 14.3 %copy-start.59 = (bf16[5106,64]{0,1:T(8,128)(2,1)S(1)}, bf16[5106,64]{0,1:T(8,128)(2,1)}, u32[]{:S(2)}) copy-start(bf16[5106,64]{0,1:T(8,128)(2,1)} %convert.43) | copy-start | bytes 1960708
  39.8 6.2 %copy-start.56 = (s32[16,1024]{1,0:T(8,128)}, s32[16,1024]{1,0:T(8,128)S(1)}, u32[]{:S(2)}) copy-start(s32[16,1024]{1,0:T(8,128)S(1)} %slice_convert_fusion) | copy-start | bytes 196612
  67.8 12.9 %copy-start.45 = (bf16[128,1024]{1,0:T(8,128)(2,1)}, bf16[128,1024]{1,0:T(8,128)(2,1)S(1)}, u32[]{:S(2)}) copy-start(bf16[128,1024]{1,0:T(8,128)(2,1)S(1)} %add_convert_fusion.1) | copy-start | bytes 786436
  67.8 8.2 %collective-permute-start.2 = (bf16[128,1024]{1,0:T(8,128)(2,1)S(1)}, bf16[128,1024]{1,0:T(8,128)(2,1)S(1)}, u32[]{:S(2)}, u32[]{:S(2)}) collective-permute-start(bf16[128,1024]{1,0:T(8,128)(2,1)S(1)} %add_convert_fusion.1), channel_id=1, source_target_pairs={{0,2},{2,0},{1,3},{3,1},{4,6},{6,4},{5,7},{7,5},{8,10},{10,8},{9,1... | collective-permute-start | bytes 786440 | tf_op jit(solution)/shard_map/ppermute | solution.py:201
  72.1 422.0 %reduce-scatter.2.cloned.1.call-start = ((), (), s32[]{:S(2)}) async-start(), calls=%async_computation.4 | async-start | bytes 4718592 | tf_op jit(solution)/shard_map/reduce_scatter | solution.py:1275
  76.1 2.0 collective-permute-start.3
  76.4 37.9 %copy-start.33 = (s32[8]{0:T(128)}, s32[8]{0:T(128)S(1)}, u32[]{:S(2)}) copy-start(s32[8]{0:T(128)S(1)} %and_select_fusion.3.limit_ref) | copy-start | bytes 100
  172.9 4.9 copy-start.10
  172.9 4.9 copy-start.95
  218.7 1.2 collective-permute-start.4
  220.0 4.2 collective-permute-start.5
  229.1 30.9 %copy-start.99 = (f32[512,1024]{1,0:T(8,128)S(1)}, f32[512,1024]{1,0:T(8,128)}, u32[]{:S(2)}) copy-start(f32[512,1024]{1,0:T(8,128)} %get-tuple-element.232) | copy-start | bytes 6291460
  230.4 29.5 %copy-start.96 = (bf16[1024,2048]{1,0:T(8,128)(2,1)S(1)}, bf16[1024,2048]{1,0:T(8,128)(2,1)}, u32[]{:S(2)}) copy-start(bf16[1024,2048]{1,0:T(8,128)(2,1)} %all-gather.6.cloned.1.call-done) | copy-start | bytes 12582916
  269.7 4.8 copy-start.15
  277.5 23.9 %copy-start.32 = (f32[6,1024]{1,0:T(8,128)S(1)}, f32[6,1024]{1,0:T(8,128)}, u32[]{:S(2)}) copy-start(f32[6,1024]{1,0:T(8,128)} %copy-done.31) | copy-start | bytes 73732
  300.1 4.7 copy-start.23
  300.1 17.1 %copy-start.3 = (bf16[3,64,2048]{2,1,0:T(8,128)(2,1)S(1)}, bf16[3,64,2048]{2,1,0:T(8,128)(2,1)}, u32[]{:S(2)}) copy-start(bf16[3,64,2048]{2,1,0:T(8,128)(2,1)} %get-tuple-element.67.q_ref.k_ref.v_ref) | copy-start | bytes 2359300
  318.8 18.4 %copy-start.73 = (f32[1,1,2048]{2,1,0:T(1,128)S(1)}, f32[1,1,2048]{2,1,0:T(1,128)}, u32[]{:S(2)}) copy-start(f32[1,1,2048]{2,1,0:T(1,128)} %get-tuple-element.183) | copy-start | bytes 24580
  318.8 18.4 %copy-start.74 = (f32[1,1,2048]{2,1,0:T(1,128)S(1)}, f32[1,1,2048]{2,1,0:T(1,128)}, u32[]{:S(2)}) copy-start(f32[1,1,2048]{2,1,0:T(1,128)} %get-tuple-element.184) | copy-start | bytes 24580
  369.3 42.3 %copy-start.5 = (bf16[3,4,64,512]{3,2,1,0:T(8,128)(2,1)S(1)}, bf16[3,4,64,512]{3,2,1,0:T(8,128)(2,1)}, u32[]{:S(2)}) copy-start(bf16[3,4,64,512]{3,2,1,0:T(8,128)(2,1)} %pairs_6.1) | copy-start | bytes 2359300
  369.3 42.6 %copy-start.71 = (f32[4,1024]{1,0:T(4,128)S(1)}, f32[4,1024]{1,0:T(4,128)}, u32[]{:S(2)}) copy-start(f32[4,1024]{1,0:T(4,128)} %slice.373) | copy-start | bytes 49156
  369.3 42.6 %copy-start.72 = (f32[4,1024]{1,0:T(4,128)S(1)}, f32[4,1024]{1,0:T(4,128)}, u32[]{:S(2)}) copy-start(f32[4,1024]{1,0:T(4,128)} %slice.375) | copy-start | bytes 49156
  369.3 42.6 %copy-start.75 = (f32[2,1024]{1,0:T(2,128)S(1)}, f32[2,1024]{1,0:T(2,128)}, u32[]{:S(2)}) copy-start(f32[2,1024]{1,0:T(2,128)} %slice.372) | copy-start | bytes 24580
  369.3 42.6 %copy-start.76 = (f32[2,1024]{1,0:T(2,128)S(1)}, f32[2,1024]{1,0:T(2,128)}, u32[]{:S(2)}) copy-start(f32[2,1024]{1,0:T(2,128)} %slice.374) | copy-start | bytes 24580
  415.5 65.2 %copy-start.81 = (f32[64]{0:T(128)S(1)}, f32[64]{0:T(128)}, u32[]{:S(2)}) copy-start(f32[64]{0:T(128)} %get-tuple-element.219) | copy-start | bytes 772
  415.5 65.2 %copy-start.82 = (f32[64]{0:T(128)S(1)}, f32[64]{0:T(128)}, u32[]{:S(2)}) copy-start(f32[64]{0:T(128)} %get-tuple-element.220) | copy-start | bytes 772
  415.5 65.2 %copy-start.83 = (f32[64]{0:T(128)S(1)}, f32[64]{0:T(128)}, u32[]{:S(2)}) copy-start(f32[64]{0:T(128)} %get-tuple-element.221) | copy-start | bytes 772
  415.5 65.2 %copy-start.84 = (f32[64]{0:T(128)S(1)}, f32[64]{0:T(128)}, u32[]{:S(2)}) copy-start(f32[64]{0:T(128)} %get-tuple-element.222) | copy-start | bytes 772
  480.7 4.6 copy-start.65
  480.7 4.6 copy-start.67
  491.9 6.7 %copy-start.94 = (pred[128]{0:T(512)(128)(4,1)S(1)}, pred[128]{0:T(512)(128)(4,1)}, u32[]{:S(2)}) copy-start(pred[128]{0:T(512)(128)(4,1)} %iota_compare_fusion.15) | copy-start | bytes 388
  517.2 13.4 %collective-permute-start.6 = (f32[64,2048]{1,0:T(8,128)S(1)}, f32[64,2048]{1,0:T(8,128)S(1)}, u32[]{:S(2)}, u32[]{:S(2)}) collective-permute-start(f32[64,2048]{1,0:T(8,128)S(1)} %get-tuple-element.142), channel_id=1, source_target_pairs={{0,1},{1,0},{2,3},{3,2},{4,5},{5,4},{6,7},{7,6},{8,9},{9,8},{10,11... | collective-permute-start | bytes 1572872 | tf_op jit(solution)/shard_map/ppermute | solution.py:201
  522.3 4.5 copy-start.78
  522.3 4.5 copy-start.89
  522.3 4.5 copy-start.90
  522.4 5.1 copy-start.47
  522.4 5.1 copy-start.60
  522.4 5.1 copy-start.61
  (63 other events, 141.1 us)
Sparse Core Ops, SparseCore 0:
  11.6 60.5 all-gather.3
  74.9 87.8 all-gather.5
  165.5 48.1 all-gather.7
  269.8 106.0 reduce-scatter.1

commit v2 on v1

--- a/solution.py
+++ b/solution.py
@@ -839,7 +839,7 @@
 
 
 def chunks(total):
-    return min(total, 512)
+    return min(total, 1024)
 
 
 def forward_kernel(

time: 549 us -> 548 us (level)
  transfers between devices with their start and end apart: 11 -> 11, of which waited for: 6 -> 6; matrix products, arithmetic and copies ran while one was open for 16% -> 16% of each run, Pallas kernels for 59% -> 58%
where the time goes in v2:
time: 548 us; the launch traced here: 543 us
  Pallas kernels  364 us (66%)
  other arithmetic  49.3 us (9%)
  local copies, waits for them, and re-layouts  44.8 us (8%)
  matrix products  33.6 us (6%)
  between operations  24.8 us (5%)
  waiting for transfers between devices  20.5 us (4%)
    pallas_call x5, Pallas kernels, stage(): pl.pallas_call(functools.partial(stage_kernel, mode, parts, items, sizes,...  138 us
    pallas_call x4, Pallas kernels, pair_exchange(): pl.pallas_call(functools.partial(pairs_kernel, sizes, heads, tokens, outw...  88.8 us
    pallas_call x1, Pallas kernels, tail_stage(): pl.pallas_call(functools.partial(tail_kernel, items, sizes), out_shape=sh...  65.1 us
    pallas_call x3, Pallas kernels, direct(): pl.pallas_call(functools.partial(direct_kernel, axes, sizes, spreads), ou...  42.3 us
    dot_general x16, matrix products, contract(): lax.dot_general(left, right, (((left_dim,), (right_dim,)), ((), ())), pre...  33.6 us
    unnamed x218, local copies, waits for them, and re-layouts  21.7 us
    pallas_call x1, Pallas kernels, attend_backward(): pl.pallas_call(backward_kernel, grid=(queries // width,), out_shape=(jax....  14.4 us
    all_gather x3, waiting for transfers between devices, everywhere(): return lax.all_gather(block, 'seq', axis=0, tiled=True)  12.4 us
  transfers between devices with their start and end apart: 11, of which 6 were waited for; matrix products, arithmetic and copies ran while one was open for 16% of the time, Pallas kernels for 58%

profile of v2, /device:TPU:0, one launch (start us, length us, event | category | flops | bytes accessed | tf_op | source)
XLA Modules:
  0.0 542.6 jit_solution(14177166987427987836)
XLA Ops:
  20.5 1.9 iota_compare_fusion.11
  22.3 1.9 iota_compare_fusion.13
  27.1 11.6 %direct_1.1 = f32[16,8,512]{2,1,0:T(8,128)} custom-call(f32[16,8,512]{2,1,0:T(8,128)} %pad_maximum_fusion.5.refs_0_), custom_call_target="tpu_custom_call" | custom-call | tf_op jit(solution)/shard_map/direct_1/pallas_call | solution.py:103
  40.3 5.7 %fusion.28 = bf16[8,16,8,128]{3,2,1,0:T(8,128)(2,1)S(1)} fusion(s32[2048]{0:T(1024)S(1)} %bitcast.363, bf16[5106,64]{0,1:T(8,128)(2,1)S(1)} %copy-done.59), kind=kOutput, calls=%fused_computation.53 | convolution fusion | flops 1082261504 | bytes 794624 | tf_op jit(solution)/shard_map/dot_general | solution.py:1049
  47.4 16.7 %direct_2.1 = (bf16[16,64,128]{2,1,0:T(8,128)(2,1)}, f32[16,4,512]{2,1,0:T(4,128)}) custom-call(bf16[16,64,128]{2,1,0:T(8,128)(2,1)} %bitcast.302, f32[4,512]{1,0:T(4,128)} %reduce_sum.237.refs_1_), custom_call_target="tpu_custom_call" | custom-call | tf_op jit(solution)/shard_map/direct_2/pallas_call | solution.py:103
  67.8 1.7 collective-permute-start.2
  70.4 1.7 split.23
  72.2 3.8 collective-permute-done.2
  76.4 1.6 collective-permute-done.3
  78.1 2.6 fusion.25
  83.0 31.3 %pairs_3.1 = (bf16[3,64,2048]{2,1,0:T(8,128)(2,1)}, f32[1,8,2048]{2,1,0:T(8,128)}) custom-call(bf16[3,4,64,512]{3,2,1,0:T(8,128)(2,1)} %pad_maximum_fusion.1.refs_0_, f32[1,4,8,512]{3,2,1,0:T(8,128)} %maximum_bitcast_fusion.4.refs_1_), custom_call_target="tpu_custom_call" | custom-call | tf_op jit(solution)/shard_map/pairs_3/pallas_call | solution.py:185
  115.4 9.2 %attend_forward.1 = (bf16[64,2048]{1,0:T(8,128)(2,1)S(1)}, f32[1,2048]{1,0:T(1,128)S(1)}, bf16[96,2048]{1,0:T(8,128)(2,1)S(1)}, bf16[96,2048]{1,0:T(8,128)(2,1)S(1)}) custom-call(s32[8]{0:T(128)S(1)} %and_select_fusion.3.limit_ref, bf16[3,64,2048]{2,1,0:T(8,128)(2,1)S(1)} %copy-done.2, bf16[3,64,2048]{2,1,0:T(8,128)(2,1)S(1)} %copy-done.2, ...), custom_call_target="tpu_custom_call" | custom-call | tf_op jit(solution)/shard_map/attend_forward/pallas_call | solution.py:909
  125.4 19.4 %pairs_4.1 = bf16[1,4,64,512]{3,2,1,0:T(8,128)(2,1)} custom-call(bf16[1,64,2048]{2,1,0:T(8,128)(2,1)} %bitcast.291), custom_call_target="tpu_custom_call" | custom-call | tf_op jit(solution)/shard_map/pairs_4/pallas_call | solution.py:185
  145.8 1.5 fusion.46.refs_0_
  147.3 22.6 %stage_10.1 = (f32[128,1024]{1,0:T(8,128)S(1)}, f32[128,1024]{1,0:T(8,128)S(1)}, bf16[4,128,1024]{2,1,0:T(8,128)(2,1)S(1)}) custom-call(f32[4,128,1024]{2,1,0:T(8,128)S(1)} %fusion.46.refs_0_, f32[128,1024]{1,0:T(8,128)S(1)} %get-tuple-element.230.refs_1_, f32[16,1024]{1,0:T(8,128)S(1)} %get-tuple-element.177.refs_2_.refs_3_.refs_4_, ...), custom_call_target="tpu_custom_call" | custom-call | tf_op jit(solution)/shard_map/stage_10/pallas_call | solution.py:578
  170.7 5.0 multiply_convert_fusion.1
  177.0 22.6 %stage_11.1 = (f32[128,1024]{1,0:T(8,128)S(1)}, f32[128,1024]{1,0:T(8,128)S(1)}, bf16[4,128,1024]{2,1,0:T(8,128)(2,1)S(1)}) custom-call(f32[4,128,1024]{2,1,0:T(8,128)S(1)} %bitcast.279, f32[128,1024]{1,0:T(8,128)S(1)} %get-tuple-element.73.refs_1_, f32[16,1024]{1,0:T(8,128)S(1)} %get-tuple-element.177.refs_2_.refs_3_.refs_4_, ...), custom_call_target="tpu_custom_call" | custom-call | tf_op jit(solution)/shard_map/stage_11/pallas_call | solution.py:578
  201.2 12.4 %all-gather.8.cloned.1.call-done = bf16[1024,1024]{1,0:T(8,128)(2,1)} async-done(((bf16[128,1024]{1,0:T(8,128)(2,1)}), bf16[1024,1024]{1,0:T(8,128)(2,1)}) %all-gather.8.cloned.1.call-update) | async-done | bytes 2097168 | tf_op jit(solution)/shard_map/all_gather | solution.py:1119
  213.5 2.9 fusion.97
  216.5 1.3 copy-done.38
  219.9 1.6 collective-permute-start.5
  222.7 1.3 copy.133
  224.8 2.3 multiply_convert_fusion
  230.4 29.5 %stage_12.1 = (f32[128,1024]{1,0:T(8,128)S(1)}, f32[6,1024]{1,0:T(8,128)S(1)}, bf16[4,128,1024]{2,1,0:T(8,128)(2,1)S(1)}, f32[64,1024]{1,0:T(8,128)S(1)}) custom-call(f32[4,128,1024]{2,1,0:T(8,128)S(1)} %bitcast.280, f32[128,1024]{1,0:T(8,128)S(1)} %copy-done.22, f32[128,1024]{1,0:T(8,128)S(1)} %copy-done.20, ...), custom_call_target="tpu_custom_call" | custom-call | tf_op jit(solution)/shard_map/stage_12/pallas_call | solution.py:578
  259.9 2.3 fusion.9.refs_1_
  262.3 4.3 outer.2
  266.6 2.0 copy-done.4
  272.9 1.5 fusion.90
  274.4 3.0 fusion.16
  277.5 22.6 %stage_13.1 = (f32[128,1024]{1,0:T(8,128)S(1)}, f32[6,1024]{1,0:T(8,128)S(1)}, bf16[4,128,1024]{2,1,0:T(8,128)(2,1)S(1)}) custom-call(f32[4,128,1024]{2,1,0:T(8,128)S(1)} %bitcast.278, f32[128,1024]{1,0:T(8,128)S(1)} %get-tuple-element.73.refs_1_, f32[128,1024]{1,0:T(8,128)S(1)} %copy-done.18, f32[128,1024]{1,0:T(8,128)S(1)} %copy-done.26, ...), custom_call_target="tpu_custom_call" | custom-call | tf_op jit(solution)/shard_map/stage_13/pallas_call | solution.py:578
  302.5 2.3 convolution_convert_fusion
  305.7 10.6 %pairs_5.1 = bf16[1,64,2048]{2,1,0:T(8,128)(2,1)} custom-call(bf16[1,4,64,512]{3,2,1,0:T(8,128)(2,1)} %bitcast.328), custom_call_target="tpu_custom_call" | custom-call | tf_op jit(solution)/shard_map/pairs_5/pallas_call | solution.py:185
  317.9 14.4 %attend_backward.1 = (f32[64,2048]{1,0:T(8,128)S(1)}, f32[64,2048]{1,0:T(8,128)S(1)}, f32[64,2048]{1,0:T(8,128)S(1)}) custom-call(s32[8]{0:T(128)S(1)} %copy-done.34, bf16[96,2048]{1,0:T(8,128)(2,1)S(1)} %get-tuple-element.68.qa_ref, bf16[96,2048]{1,0:T(8,128)(2,1)S(1)} %get-tuple-element.69.ka_ref, bf16[3,64,2048]{2,1,0:T(8,128)(2,1)S(1)} %copy-done.3, ...), custom_call_target="tpu_custom_call" | custom-call | tf_op jit(solution)/shard_map/attend_backward/pallas_call | solution.py:994
  333.7 27.7 %pairs_6.1 = bf16[3,4,64,512]{3,2,1,0:T(8,128)(2,1)} custom-call(bf16[3,64,2048]{2,1,0:T(8,128)(2,1)} %pad_maximum_fusion.2.refs_0_), custom_call_target="tpu_custom_call" | custom-call | tf_op jit(solution)/shard_map/pairs_6/pallas_call | solution.py:185
  361.4 1.4 copy.140
  362.8 2.2 fusion.43.refs_5_
  366.1 41.2 %stage_14.1 = (f32[128,1024]{1,0:T(8,128)S(1)}, f32[4,1024]{1,0:T(4,128)S(1)}, f32[64,1024]{1,0:T(8,128)S(1)}) custom-call(f32[4,128,1024]{2,1,0:T(8,128)S(1)} %fusion.20.refs_0_, f32[128,1024]{1,0:T(8,128)S(1)} %get-tuple-element.230.refs_1_, f32[128,1024]{1,0:T(8,128)S(1)} %copy-done.24, f32[16,1024]{1,0:T(8,128)S(1)} %get-tuple-element.177.refs_2_.refs_3_.refs_4_, ...), custom_call_target="tpu_custom_call" | custom-call | tf_op jit(solution)/shard_map/stage_14/pallas_call | solution.py:578
  411.2 2.0 outer.3
  413.4 65.1 %tail_8.1 = (f32[16,2,2,512]{3,2,1,0:T(2,128)S(1)}, f32[16,3,512]{2,1,0:T(4,128)S(1)}, f32[64,2048]{1,0:T(8,128)S(1)}, f32[64,4096]{1,0:T(8,128)S(1)}, f32[64,128]{1,0:T(8,128)S(1)}) custom-call(f32[16,64,128]{2,1,0:T(8,128)S(1)} %bitcast.277, f32[16,3,512]{2,1,0:T(4,128)S(1)} %pad_maximum_fusion.7.refs_1_, f32[4,2,128,1024]{3,2,1,0:T(8,128)S(1)} %bitcast.272, ...), custom_call_target="tpu_custom_call" | custom-call | tf_op jit(solution)/shard_map/tail_8/pallas_call | solution.py:824
  478.9 3.6 multiply_reduce_fusion.4
  492.3 1.9 multiply_reduce_fusion.6
  497.4 14.1 %direct_9.1 = f32[32,8,128]{2,1,0:T(8,128)} custom-call(f32[8,128]{1,0:T(8,128)} %broadcast_select_fusion.1.refs_0_), custom_call_target="tpu_custom_call" | custom-call | tf_op jit(solution)/shard_map/direct_9/pallas_call | solution.py:103
  514.5 1.3 convert.99
  516.8 2.7 multiply_subtract_fusion.1
  521.1 4.4 multiply_subtract_fusion
  526.2 1.5 fusion.79
  527.8 1.5 fusion.75
  531.2 2.5 fusion.77
  (412 shorter events, 69.9 us)
Async XLA Ops:
  7.2 12.7 %copy-start = (s32[1,2048]{1,0:T(1,128)S(1)}, s32[1,2048]{1,0:T(1,128)}, u32[]{:S(2)}) copy-start(s32[1,2048]{1,0:T(1,128)} %param.26) | copy-start | bytes 24580
  7.2 70.8 %all-gather.4.cloned.1.call-start = ((), (), s32[]{:S(2)}) async-start(), calls=%async_computation.1 | async-start | bytes 2359296 | tf_op jit(solution)/shard_map/all_gather | solution.py:1119
  9.2 1.5 collective-permute-start
  11.4 159.3 %all-gather.6.cloned.1.call-start = ((), (), s32[]{:S(2)}) async-start(), calls=%async_computation.2 | async-start | bytes 4718592 | tf_op jit(solution)/shard_map/all_gather | solution.py:1119
  14.1 1.8 collective-permute-start.1
  16.9 9.1 %copy-start.35 = (f32[64,8192]{1,0:T(8,128)S(1)}, f32[64,8192]{1,0:T(8,128)}, u32[]{:S(2)}) copy-start(f32[64,8192]{1,0:T(8,128)} %param.31) | copy-start | bytes 6291460
  17.8 195.8 %all-gather.8.cloned.1.call-start = ((), (), s32[]{:S(2)}) async-start(), calls=%async_computation.3 | async-start | bytes 2359296 | tf_op jit(solution)/shard_map/all_gather | solution.py:1119
  18.4 7.9 %copy-start.91 = (s32[1,256]{1,0:T(1,128)S(1)}, s32[1,256]{1,0:T(1,128)}, u32[]{:S(2)}) copy-start(s32[1,256]{1,0:T(1,128)} %param.25) | copy-start | bytes 3076
  18.4 7.9 %copy-start.92 = (s32[1,256]{1,0:T(1,128)S(1)}, s32[1,256]{1,0:T(1,128)}, u32[]{:S(2)}) copy-start(s32[1,256]{1,0:T(1,128)} %param.24) | copy-start | bytes 3076
  18.4 7.9 %copy-start.93 = (s32[1,256]{1,0:T(1,128)S(1)}, s32[1,256]{1,0:T(1,128)}, u32[]{:S(2)}) copy-start(s32[1,256]{1,0:T(1,128)} %param.23) | copy-start | bytes 3076
  26.0 14.3 %copy-start.59 = (bf16[5106,64]{0,1:T(8,128)(2,1)S(1)}, bf16[5106,64]{0,1:T(8,128)(2,1)}, u32[]{:S(2)}) copy-start(bf16[5106,64]{0,1:T(8,128)(2,1)} %convert.43) | copy-start | bytes 1960708
  39.8 6.2 %copy-start.56 = (s32[16,1024]{1,0:T(8,128)}, s32[16,1024]{1,0:T(8,128)S(1)}, u32[]{:S(2)}) copy-start(s32[16,1024]{1,0:T(8,128)S(1)} %slice_convert_fusion) | copy-start | bytes 196612
  67.8 12.9 %copy-start.45 = (bf16[128,1024]{1,0:T(8,128)(2,1)}, bf16[128,1024]{1,0:T(8,128)(2,1)S(1)}, u32[]{:S(2)}) copy-start(bf16[128,1024]{1,0:T(8,128)(2,1)S(1)} %add_convert_fusion.1) | copy-start | bytes 786436
  67.8 8.2 %collective-permute-start.2 = (bf16[128,1024]{1,0:T(8,128)(2,1)S(1)}, bf16[128,1024]{1,0:T(8,128)(2,1)S(1)}, u32[]{:S(2)}, u32[]{:S(2)}) collective-permute-start(bf16[128,1024]{1,0:T(8,128)(2,1)S(1)} %add_convert_fusion.1), channel_id=1, source_target_pairs={{0,2},{2,0},{1,3},{3,1},{4,6},{6,4},{5,7},{7,5},{8,10},{10,8},{9,1... | collective-permute-start | bytes 786440 | tf_op jit(solution)/shard_map/ppermute | solution.py:201
  72.1 420.2 %reduce-scatter.2.cloned.1.call-start = ((), (), s32[]{:S(2)}) async-start(), calls=%async_computation.4 | async-start | bytes 4718592 | tf_op jit(solution)/shard_map/reduce_scatter | solution.py:1275
  76.1 2.0 collective-permute-start.3
  76.4 37.9 %copy-start.33 = (s32[8]{0:T(128)}, s32[8]{0:T(128)S(1)}, u32[]{:S(2)}) copy-start(s32[8]{0:T(128)S(1)} %and_select_fusion.3.limit_ref) | copy-start | bytes 100
  170.7 5.0 copy-start.10
  170.7 5.0 copy-start.95
  218.6 1.2 collective-permute-start.4
  219.9 4.2 collective-permute-start.5
  229.1 30.8 %copy-start.99 = (f32[512,1024]{1,0:T(8,128)S(1)}, f32[512,1024]{1,0:T(8,128)}, u32[]{:S(2)}) copy-start(f32[512,1024]{1,0:T(8,128)} %get-tuple-element.232) | copy-start | bytes 6291460
  230.4 29.5 %copy-start.96 = (bf16[1024,2048]{1,0:T(8,128)(2,1)S(1)}, bf16[1024,2048]{1,0:T(8,128)(2,1)}, u32[]{:S(2)}) copy-start(bf16[1024,2048]{1,0:T(8,128)(2,1)} %all-gather.6.cloned.1.call-done) | copy-start | bytes 12582916
  269.6 4.8 copy-start.15
  277.4 23.8 %copy-start.32 = (f32[6,1024]{1,0:T(8,128)S(1)}, f32[6,1024]{1,0:T(8,128)}, u32[]{:S(2)}) copy-start(f32[6,1024]{1,0:T(8,128)} %copy-done.31) | copy-start | bytes 73732
  300.0 4.7 copy-start.23
  300.1 16.2 %copy-start.3 = (bf16[3,64,2048]{2,1,0:T(8,128)(2,1)S(1)}, bf16[3,64,2048]{2,1,0:T(8,128)(2,1)}, u32[]{:S(2)}) copy-start(bf16[3,64,2048]{2,1,0:T(8,128)(2,1)} %get-tuple-element.67.q_ref.k_ref.v_ref) | copy-start | bytes 2359300
  317.9 14.6 %copy-start.73 = (f32[1,1,2048]{2,1,0:T(1,128)S(1)}, f32[1,1,2048]{2,1,0:T(1,128)}, u32[]{:S(2)}) copy-start(f32[1,1,2048]{2,1,0:T(1,128)} %get-tuple-element.183) | copy-start | bytes 24580
  317.9 14.6 %copy-start.74 = (f32[1,1,2048]{2,1,0:T(1,128)S(1)}, f32[1,1,2048]{2,1,0:T(1,128)}, u32[]{:S(2)}) copy-start(f32[1,1,2048]{2,1,0:T(1,128)} %get-tuple-element.184) | copy-start | bytes 24580
  366.1 43.3 %copy-start.5 = (bf16[3,4,64,512]{3,2,1,0:T(8,128)(2,1)S(1)}, bf16[3,4,64,512]{3,2,1,0:T(8,128)(2,1)}, u32[]{:S(2)}) copy-start(bf16[3,4,64,512]{3,2,1,0:T(8,128)(2,1)} %pairs_6.1) | copy-start | bytes 2359300
  366.1 43.6 %copy-start.71 = (f32[4,1024]{1,0:T(4,128)S(1)}, f32[4,1024]{1,0:T(4,128)}, u32[]{:S(2)}) copy-start(f32[4,1024]{1,0:T(4,128)} %slice.373) | copy-start | bytes 49156
  366.1 43.6 %copy-start.72 = (f32[4,1024]{1,0:T(4,128)S(1)}, f32[4,1024]{1,0:T(4,128)}, u32[]{:S(2)}) copy-start(f32[4,1024]{1,0:T(4,128)} %slice.375) | copy-start | bytes 49156
  366.1 43.6 %copy-start.75 = (f32[2,1024]{1,0:T(2,128)S(1)}, f32[2,1024]{1,0:T(2,128)}, u32[]{:S(2)}) copy-start(f32[2,1024]{1,0:T(2,128)} %slice.372) | copy-start | bytes 24580
  366.1 43.6 %copy-start.76 = (f32[2,1024]{1,0:T(2,128)S(1)}, f32[2,1024]{1,0:T(2,128)}, u32[]{:S(2)}) copy-start(f32[2,1024]{1,0:T(2,128)} %slice.374) | copy-start | bytes 24580
  413.3 65.6 %copy-start.81 = (f32[64]{0:T(128)S(1)}, f32[64]{0:T(128)}, u32[]{:S(2)}) copy-start(f32[64]{0:T(128)} %get-tuple-element.219) | copy-start | bytes 772
  413.3 65.6 %copy-start.82 = (f32[64]{0:T(128)S(1)}, f32[64]{0:T(128)}, u32[]{:S(2)}) copy-start(f32[64]{0:T(128)} %get-tuple-element.220) | copy-start | bytes 772
  413.3 65.6 %copy-start.83 = (f32[64]{0:T(128)S(1)}, f32[64]{0:T(128)}, u32[]{:S(2)}) copy-start(f32[64]{0:T(128)} %get-tuple-element.221) | copy-start | bytes 772
  413.4 65.6 %copy-start.84 = (f32[64]{0:T(128)S(1)}, f32[64]{0:T(128)}, u32[]{:S(2)}) copy-start(f32[64]{0:T(128)} %get-tuple-element.222) | copy-start | bytes 772
  478.9 4.6 copy-start.65
  478.9 4.6 copy-start.67
  490.1 6.7 %copy-start.94 = (pred[128]{0:T(512)(128)(4,1)S(1)}, pred[128]{0:T(512)(128)(4,1)}, u32[]{:S(2)}) copy-start(pred[128]{0:T(512)(128)(4,1)} %iota_compare_fusion.15) | copy-start | bytes 388
  515.9 13.4 %collective-permute-start.6 = (f32[64,2048]{1,0:T(8,128)S(1)}, f32[64,2048]{1,0:T(8,128)S(1)}, u32[]{:S(2)}, u32[]{:S(2)}) collective-permute-start(f32[64,2048]{1,0:T(8,128)S(1)} %get-tuple-element.142), channel_id=1, source_target_pairs={{0,1},{1,0},{2,3},{3,2},{4,5},{5,4},{6,7},{7,6},{8,9},{9,8},{10,11... | collective-permute-start | bytes 1572872 | tf_op jit(solution)/shard_map/ppermute | solution.py:201
  521.0 4.5 copy-start.78
  521.0 4.5 copy-start.89
  521.0 4.5 copy-start.90
  521.0 5.1 copy-start.47
  521.1 5.1 copy-start.60
  521.1 5.1 copy-start.61
  (63 other events, 141.3 us)
Sparse Core Ops, SparseCore 0:
  11.6 60.5 all-gather.3
  74.9 87.7 all-gather.5
  165.4 48.1 all-gather.7
  269.7 104.9 reduce-scatter.1
